TPU v7x, 256 devices: a whole 4x4x8 slice. The times are simulated.
256 devices in a mesh: gx: 8 (over x, core), gy: 32 (over y, z).
Axes of the slice: x: 4, y: 4, z: 8, core: 2. Of those that a mesh axis runs over, the one named last changes fastest.
Arguments:
- rhs: float32 [64, 64, 128, 128], P(None, 'gx', 'gy'), may hold values from -1.5 to 1.5
- coef_x: float32 [3, 64, 128, 128], P(None, 'gx', 'gy'), may hold values from 0 to 10, as said below
- coef_y: float32 [3, 64, 128, 128], P(None, 'gx', 'gy'), may hold values from 0 to 10, as said below
- out_coupling_x: float32 [64, 64], replicated, may hold values from -2 to 2
- in_coupling_x: float32 [64, 64], replicated, may hold values from -2 to 2
- inverse_x: float32 [64, 64], replicated, may hold values from -2 to 2
- boundary_inverse: float32 [3, 64, 64], replicated, may hold values from -2 to 2
- out_coupling_y: float32 [64, 64], replicated, may hold values from -2 to 2
- in_coupling_y: float32 [64, 64], replicated, may hold values from -2 to 2
- inverse_y: float32 [64, 64], replicated, may hold values from -2 to 2
- bc_flags: int32 [128, 128], P('gy'), may hold values from 0 to 2
- line_order: int32 [64, 128], P('gx'), may hold values from 0 to 1
Outputs:
- adjoint: float32 [64, 64, 128, 128], P(None, 'gx', 'gy')
Inputs may be any that keep to these rules, and one draw needn't show every extreme that they name: `coef_x`: components 0 and 1 lie strictly between 0 and 1, component 2 between 2 and 10. `coef_y`: components 0 and 1 lie strictly between 0 and 1, component 2 between 2 and 10.
All inputs are finite; a program needn't handle non-finite values.
Results may differ from a plain program's by a relative error of at most 0.0002.
Values sent between devices are 32-bit elements; how exact they have to be, the bound alone decides.
No kernel may reach another device: no remote copies, remote signals or barrier semaphores. Data moves between devices by JAX's collectives and lax.ppermute only.
A program may use at most 128 MiB of HBM per device.

v0:
```python
import functools

import jax
import jax.numpy as jnp
from jax import lax
from jax.experimental import pallas as pl
from jax.experimental.pallas import tpu as pltpu
from jax.sharding import PartitionSpec as P

NP = 64
LANES = 128
CX = 8
CY = 4
SX = 8
SY = 32
F32 = jnp.float32
BF16 = jnp.bfloat16
VMEM_LIMIT = 48 * 1024 * 1024


def rounded(v):
    return v.astype(BF16).astype(F32)


def split_matrix(m):
    high = rounded(m)
    rest = m - high
    mid = rounded(rest)
    low = rest - mid
    part = lax.broadcasted_iota(jnp.int32, m.shape, 1) // NP
    return jnp.where(part == 1, mid, jnp.where(part == 3, low, high)).astype(BF16)


def split_vectors(v):
    high = v.astype(BF16)
    low = (v - high.astype(F32)).astype(BF16)
    return jnp.concatenate([high, high, low, high], axis=0)


def product(parts, vectors):
    return jnp.dot(parts, vectors, preferred_element_type=F32)


def apply(parts, v):
    return product(parts, split_vectors(v))


def lane_iota(shape):
    return lax.broadcasted_iota(jnp.int32, shape, len(shape) - 1)


def roll(v, shift):
    shift = shift % LANES
    return v if shift == 0 else pltpu.roll(v, shift, 1)


def row_of(block):
    return jnp.concatenate([block[r : r + 1] for r in range(block.shape[0])], axis=1)


def columns(v):
    return [v[:, LANES * j : LANES * (j + 1)] for j in range(v.shape[1] // LANES)]


def regroup(blocks, width):
    n = LANES // width
    rolled = [[roll(b, width * k) for k in range(n)] for b in blocks]
    group = lane_iota(blocks[0].shape) // width
    outs = []
    for a in range(n):
        acc = rolled[0][(0 - a) % n]
        for q in range(1, n):
            acc = jnp.where(group == q, rolled[q][(q - a) % n], acc)
        outs.append(acc)
    return outs


def replicate(block, width):
    return regroup([block] * (LANES // width), width)


def shifted(v, t, width, ncol, reverse):
    cols = columns(v)
    group = lane_iota(cols[0].shape) // width
    n = LANES // width
    out = []
    for j in range(ncol):
        k = j + t if reverse else j - t
        carry = abs(k // ncol)
        src = cols[k % ncol]
        if carry:
            if reverse:
                src = jnp.where(group < n - carry, roll(src, -width * carry), 0.0)
            else:
                src = jnp.where(group >= carry, roll(src, width * carry), 0.0)
        out.append(src)
    return jnp.concatenate(out, axis=1)


def scan_segments(v, rate, powers, width, ncol, reverse):
    for k in range(powers.shape[0]):
        t = 1 << k
        v = v + rate * apply(powers[k], shifted(v, t, width, ncol, reverse))
        if k + 1 < powers.shape[0]:
            rate = rate * shifted(rate, t, width, ncol, reverse)
    return v


def x_sweep(rank, load, coef_ref, flags_ref, both, down, bounds, scaled_ref, enter, leave, store):
    def rates(which, i):
        return row_of(coef_ref[which, CY * i : CY * (i + 1), :])

    flags = row_of(flags_ref[...])
    carry = enter
    for i in range(CX):
        f = load(i)
        if carry is not None:
            f = f + carry
        vectors = split_vectors(f)
        out = product(both, vectors)
        carry = rates(1, i) * out[:NP]
        scaled = out[NP:]
        if i == 0 or i == CX - 1:
            ends = product(bounds, vectors)
            chosen = jnp.where(
                flags == 0, ends[:NP], jnp.where(flags == 1, ends[NP : 2 * NP], ends[2 * NP :])
            )
            scaled = jnp.where(rank == (0 if i == 0 else SX - 1), chosen, scaled)
        scaled_ref[i] = scaled * (1.0 / rates(2, i))
    outgoing = carry
    carry = leave
    for i in reversed(range(CX)):
        g = scaled_ref[i]
        if carry is not None:
            g = g + carry
        if store is not None:
            store(i, g)
        if store is None or i > 0:
            carry = rates(0, i) * apply(down, g)
    return outgoing, carry


def x_local_kernel(rank_ref, rhs_ref, coef_ref, flags_ref, mats_ref, out_ref, scaled_ref):
    rank = rank_ref[0]
    parts = split_matrix(mats_ref[0 : 6 * NP])
    both, down, bounds = parts[: 2 * NP], parts[2 * NP : 3 * NP], parts[3 * NP :]

    def load(i):
        return jnp.concatenate(
            [rhs_ref[pl.ds(CY * i + y, NP, stride=CX * CY), :] for y in range(CY)], axis=1
        )

    f, g = x_sweep(
        rank, load, coef_ref, flags_ref, both, down, bounds, scaled_ref, None, None, None
    )
    for y, (fy, gy) in enumerate(zip(columns(f), columns(g))):
        even, odd = regroup([fy, gy], NP)
        out_ref[2 * y, 0:NP, :] = even
        out_ref[2 * y + 1, 0:NP, :] = odd
    down_rate = coef_ref[0, 0:CY, :]
    up_rate = jnp.ones_like(down_rate)
    gains = []
    for i in range(CX):
        gains.append(down_rate * up_rate / coef_ref[2, CY * i : CY * (i + 1), :])
        up_rate = up_rate * coef_ref[1, CY * i : CY * (i + 1), :]
        if i + 1 < CX:
            down_rate = down_rate * coef_ref[0, CY * (i + 1) : CY * (i + 2), :]
    last = gains.pop()
    is_last = rank == SX - 1
    flags = flags_ref[...]
    gains.append(jnp.where(is_last, 0.0, last))
    for kind in range(3):
        gains.append(jnp.where(jnp.logical_and(is_last, flags == kind), last, 0.0))
    values = [up_rate, down_rate] + gains + [jnp.zeros_like(last)] * 3
    for r in range(8):
        even, odd = regroup([values[2 * r], values[2 * r + 1]], NP)
        for y in range(CY):
            out_ref[2 * y, NP + r : NP + r + 1, :] = even[y : y + 1]
            out_ref[2 * y + 1, NP + r : NP + r + 1, :] = odd[y : y + 1]


def x_owner_kernel(in_ref, gain_ref, up_ref, down_ref, norm_ref, out_ref):
    half = SX // 2
    fs, gs, sa, sb = [], [], [], []
    for j in range(half):
        f, g = regroup([in_ref[j], in_ref[half + j]], NP)
        fs.append(f[:NP])
        gs.append(g[:NP])
        sa.append(f[NP:])
        sb.append(g[NP:])
    f = jnp.concatenate(fs, axis=1)
    g = jnp.concatenate(gs, axis=1)
    even = jnp.concatenate(sa, axis=1)
    odd = jnp.concatenate(sb, axis=1)
    scalar = [(even if k % 2 == 0 else odd)[k // 2 : k // 2 + 1] for k in range(13)]
    width, ncol = NP, half
    up_rate = scalar[0] * norm_ref[0:1, 0:1]
    down_rate = scalar[1] * norm_ref[1:2, 0:1]
    h = scan_segments(
        shifted(f, 1, width, ncol, False),
        shifted(up_rate, 1, width, ncol, False),
        up_ref,
        width,
        ncol,
        False,
    )
    vectors = split_vectors(h)
    through = product(gain_ref[0 : CX * NP], vectors)
    for i in range(CX):
        g = g + scalar[2 + i] * through[NP * i : NP * (i + 1)]
    ends = product(gain_ref[CX * NP :], vectors[:, LANES * (half - 1) :])
    extra = 0.0
    for kind in range(3):
        extra = extra + (
            scalar[10 + kind][:, LANES * (half - 1) :] * ends[NP * kind : NP * (kind + 1)]
        )
    g = jnp.concatenate([g[:, : LANES * (half - 1)], g[:, LANES * (half - 1) :] + extra], axis=1)
    e = scan_segments(
        shifted(g, 1, width, ncol, True),
        shifted(down_rate, 1, width, ncol, True),
        down_ref,
        width,
        ncol,
        True,
    )
    for j, (hj, ej) in enumerate(zip(columns(h), columns(e))):
        first, second = regroup([hj, ej], NP)
        out_ref[j] = first
        out_ref[half + j] = second


def y_rates(coef_ref, which, flip, p):
    here = coef_ref[which, pl.ds(p, CX, stride=CY), :]
    there = coef_ref[which, pl.ds(CY - 1 - p, CX, stride=CY), :]
    return jnp.where(flip, there, here)


def y_sweep(load, rates, both, down, enter, leave, scaled_ref, store):
    carry = enter
    for p in range(CY):
        f = load(p)
        if carry is not None:
            f = f + carry
        out = apply(both, f)
        carry = row_of(rates(1, p)) * out[:NP]
        scaled_ref[p] = out[NP:] * row_of(1.0 / rates(2, p))
    outgoing = carry
    carry = leave
    for p in reversed(range(CY)):
        g = scaled_ref[p]
        if carry is not None:
            g = g + carry
        if store is not None:
            store(p, g)
        if store is None or p > 0:
            carry = row_of(rates(0, p)) * apply(down, g)
    return outgoing, carry


def middle_kernel(
    rank_ref,
    rhs_ref,
    coef_ref,
    flags_ref,
    mats_ref,
    in_ref,
    coef_y_ref,
    order_ref,
    adj_ref,
    out_ref,
    scaled_ref,
    scaled_y_ref,
):
    rank = rank_ref[0]
    parts = split_matrix(mats_ref[...])
    both, down, bounds = parts[: 2 * NP], parts[2 * NP : 3 * NP], parts[3 * NP : 6 * NP]

    def load(i):
        return jnp.concatenate(
            [rhs_ref[pl.ds(CY * i + y, NP, stride=CX * CY), :] for y in range(CY)], axis=1
        )

    hs, es = [], []
    for y in range(CY):
        h, e = regroup([in_ref[2 * y], in_ref[2 * y + 1]], NP)
        hs.append(h)
        es.append(e)

    def store(i, g):
        for y in range(CY):
            adj_ref[y, :, LANES * i : LANES * (i + 1)] = g[:, LANES * y : LANES * (y + 1)]

    x_sweep(
        rank,
        load,
        coef_ref,
        flags_ref,
        both,
        down,
        bounds,
        scaled_ref,
        jnp.concatenate(hs, axis=1),
        jnp.concatenate(es, axis=1),
        store,
    )
    both_y, down_y = parts[6 * NP : 8 * NP], parts[8 * NP :]
    flip = order_ref[...] > 0
    flip_row = row_of(order_ref[...]) > 0

    def load_y(p):
        return jnp.where(flip_row, adj_ref[CY - 1 - p], adj_ref[p])

    rates = functools.partial(y_rates, coef_y_ref)

    def oriented(which, p):
        return rates(which, flip, p)

    f, g = y_sweep(load_y, oriented, both_y, down_y, None, None, scaled_y_ref, None)
    for x, (fx, gx) in enumerate(zip(columns(f), columns(g))):
        chunks = regroup([fx[:32], fx[32:], gx[:32], gx[32:]], 32)
        for a in range(4):
            out_ref[4 * x + a, 0:32, :] = chunks[a]
    down_rate = oriented(0, 0)
    up_rate = jnp.ones_like(down_rate)
    gains = []
    for p in range(CY):
        gains.append(down_rate * up_rate / oriented(2, p))
        up_rate = up_rate * oriented(1, p)
        if p + 1 < CY:
            down_rate = down_rate * oriented(0, p + 1)
    values = [up_rate, down_rate] + gains + [flip.astype(F32), jnp.zeros_like(up_rate)]
    for r, value in enumerate(values):
        for a, block in enumerate(replicate(value, 32)):
            for x in range(CX):
                out_ref[4 * x + a, 32 + r : 33 + r, :] = block[x : x + 1]


def y_owner_kernel(in_ref, gain_ref, up_ref, down_ref, norm_ref, out_ref, res_ref):
    width, ncol = 32, 8
    flip = in_ref[0, 38:39, :] > 0.5

    def oriented(s):
        return jnp.where(flip, in_ref[SY - 1 - s], in_ref[s])

    fs, gs, ss = [], [], []
    for j in range(ncol):
        blocks = [oriented(ncol * a + j) for a in range(4)]
        outs = regroup([b[:32] for b in blocks], width)
        fs.append(jnp.concatenate(outs[:2], axis=0))
        gs.append(jnp.concatenate(outs[2:], axis=0))
        group = lane_iota((8, LANES)) // width
        acc = blocks[0][32:40]
        for a in range(1, 4):
            acc = jnp.where(group == a, blocks[a][32:40], acc)
        ss.append(acc)
    f = jnp.concatenate(fs, axis=1)
    g = jnp.concatenate(gs, axis=1)
    scalars = jnp.concatenate(ss, axis=1)
    up_rate = scalars[0:1] * norm_ref[0:1, 0:1]
    down_rate = scalars[1:2] * norm_ref[1:2, 0:1]
    h = scan_segments(
        shifted(f, 1, width, ncol, False),
        shifted(up_rate, 1, width, ncol, False),
        up_ref,
        width,
        ncol,
        False,
    )
    through = apply(gain_ref[...], h)
    for p in range(CY):
        g = g + scalars[2 + p : 3 + p] * through[NP * p : NP * (p + 1)]
    e = scan_segments(
        shifted(g, 1, width, ncol, True),
        shifted(down_rate, 1, width, ncol, True),
        down_ref,
        width,
        ncol,
        True,
    )
    for j, (hj, ej) in enumerate(zip(columns(h), columns(e))):
        outs = regroup([hj[:32], hj[32:], ej[:32], ej[32:]], width)
        for a in range(4):
            res_ref[ncol * a + j] = outs[a]
    for s in range(SY):
        out_ref[s] = jnp.where(flip, res_ref[SY - 1 - s], res_ref[s])


def y_final_kernel(adj_ref, coef_y_ref, order_ref, mats_ref, in_ref, out_ref, scaled_ref, solved_ref):
    parts = split_matrix(mats_ref[6 * NP :])
    both, down = parts[: 2 * NP], parts[2 * NP :]
    flip = order_ref[...] > 0
    flip_row = row_of(order_ref[...]) > 0
    hs, es = [], []
    for x in range(CX):
        outs = regroup([in_ref[4 * x + a] for a in range(4)], 32)
        hs.append(jnp.concatenate(outs[:2], axis=0))
        es.append(jnp.concatenate(outs[2:], axis=0))

    def load(p):
        return jnp.where(flip_row, adj_ref[CY - 1 - p], adj_ref[p])

    def store(p, g):
        solved_ref[p] = g

    y_sweep(
        load,
        lambda which, p: y_rates(coef_y_ref, which, flip, p),
        both,
        down,
        jnp.concatenate(hs, axis=1),
        jnp.concatenate(es, axis=1),
        scaled_ref,
        store,
    )
    for y in range(CY):
        plane = jnp.where(flip_row, solved_ref[CY - 1 - y], solved_ref[y])
        for x, block in enumerate(columns(plane)):
            out_ref[pl.ds(CY * x + y, NP, stride=CX * CY), :] = block


def precise(a, b):
    return jnp.dot(a[:, :NP], b, precision=lax.Precision.HIGHEST, preferred_element_type=F32)


def prepare(cells, doublings, up, down, scale, bounds, gain_ref, up_ref, down_ref, norm_ref):
    halves = cells.bit_length() - 1
    ups, downs = [up], [down]
    for _ in range(halves):
        ups.append(precise(ups[-1], ups[-1]))
        downs.append(precise(downs[-1], downs[-1]))
    scaled = scale
    stack = down
    for k in range(halves):
        scaled = jnp.concatenate([scaled, precise(scaled, ups[k])], axis=0)
        stack = jnp.concatenate([stack, precise(stack, downs[k])], axis=0)
    for j in range(cells):
        rows = slice(NP * j, NP * (j + 1))
        gain_ref[rows, :] = split_matrix(precise(stack[rows], scaled[rows]))
    if bounds is not None:
        for k in range(halves):
            bounds = precise(bounds, ups[k])
        for kind in range(3):
            rows = slice(NP * (cells + kind), NP * (cells + kind + 1))
            ends = bounds[NP * kind : NP * (kind + 1)]
            gain_ref[rows, :] = split_matrix(precise(downs[halves], ends))
    norm_ref[...] = jnp.zeros(norm_ref.shape, F32)
    for row, (power, ref) in enumerate(((ups[halves], up_ref), (downs[halves], down_ref))):
        norm = jnp.max(jnp.sum(jnp.abs(power[:, :NP]), axis=1, keepdims=True), axis=0, keepdims=True)
        norm = jnp.maximum(norm, 1e-30)
        norm_ref[row : row + 1, :] = jnp.broadcast_to(norm, (1, LANES))
        power = power / norm
        for k in range(doublings):
            ref[k] = split_matrix(power)
            if k + 1 < doublings:
                power = precise(power, power)


def prepare_x_kernel(mats_ref, gain_ref, up_ref, down_ref, norm_ref):
    prepare(
        CX,
        3,
        mats_ref[0:NP],
        mats_ref[2 * NP : 3 * NP],
        mats_ref[NP : 2 * NP],
        mats_ref[3 * NP : 6 * NP],
        gain_ref,
        up_ref,
        down_ref,
        norm_ref,
    )


def prepare_y_kernel(mats_ref, gain_ref, up_ref, down_ref, norm_ref):
    prepare(
        CY,
        5,
        mats_ref[6 * NP : 7 * NP],
        mats_ref[8 * NP : 9 * NP],
        mats_ref[7 * NP : 8 * NP],
        None,
        gain_ref,
        up_ref,
        down_ref,
        norm_ref,
    )


def shape(*dims, dtype=F32):
    return jax.ShapeDtypeStruct(dims, dtype)


def call(kernel, out_shape, n_in, scratch=(), scalars=0):
    whole = pl.BlockSpec(memory_space=pltpu.VMEM)
    specs = [pl.BlockSpec(memory_space=pltpu.SMEM)] * scalars + [whole] * n_in
    outs = jax.tree.map(lambda _: whole, out_shape)
    return pl.pallas_call(
        kernel,
        out_shape=out_shape,
        in_specs=specs,
        out_specs=outs,
        scratch_shapes=list(scratch),
        compiler_params=pltpu.CompilerParams(vmem_limit_bytes=VMEM_LIMIT),
    )


def prepared(kernel, gains, doublings, mats):
    outs = (
        shape(gains * NP, 4 * NP, dtype=BF16),
        shape(doublings, NP, 4 * NP, dtype=BF16),
        shape(doublings, NP, 4 * NP, dtype=BF16),
        shape(8, LANES),
    )
    return call(kernel, outs, 1)(mats)


def per_device(
    rhs,
    coef_x,
    coef_y,
    out_coupling_x,
    in_coupling_x,
    inverse_x,
    boundary_inverse,
    out_coupling_y,
    in_coupling_y,
    inverse_y,
    bc_flags,
    line_order,
):
    rank = lax.axis_index("gx").astype(jnp.int32).reshape(1)
    mats = jnp.concatenate(
        [
            jnp.stack([out_coupling_x, inverse_x, in_coupling_x]),
            boundary_inverse,
            jnp.stack([out_coupling_y, inverse_y, in_coupling_y]),
        ],
        0,
    )
    mats = jnp.swapaxes(mats, 1, 2).reshape(9 * NP, NP)
    mats = jnp.concatenate([mats] * 4, axis=1)
    rhs = rhs.reshape(NP * CX * CY, LANES)
    coef_x = coef_x.reshape(3, CX * CY, LANES)
    coef_y = coef_y.reshape(3, CX * CY, LANES)

    sent = call(
        x_local_kernel,
        shape(SX, NP + 8, LANES),
        4,
        [pltpu.VMEM((CX, NP, CY * LANES), F32)],
        1,
    )(rank, rhs, coef_x, bc_flags, mats)
    got = lax.all_to_all(sent, "gx", 0, 0, tiled=True)
    prep_x = prepared(prepare_x_kernel, CX + 3, 3, mats)
    back = call(x_owner_kernel, shape(SX, NP, LANES), 5)(got, *prep_x)
    terms = lax.all_to_all(back, "gx", 0, 0, tiled=True)
    prep_y = prepared(prepare_y_kernel, CY, 5, mats)
    adj, sent = call(
        middle_kernel,
        (shape(CY, NP, CX * LANES), shape(SY, 40, LANES)),
        7,
        [
            pltpu.VMEM((CX, NP, CY * LANES), F32),
            pltpu.VMEM((CY, NP, CX * LANES), F32),
        ],
        1,
    )(rank, rhs, coef_x, bc_flags, mats, terms, coef_y, line_order)
    got = lax.all_to_all(sent, "gy", 0, 0, tiled=True)
    back = call(
        y_owner_kernel, shape(SY, 32, LANES), 5, [pltpu.VMEM((SY, 32, LANES), F32)]
    )(got, *prep_y)
    terms = lax.all_to_all(back, "gy", 0, 0, tiled=True)
    out = call(
        y_final_kernel,
        shape(NP * CX * CY, LANES),
        5,
        [
            pltpu.VMEM((CY, NP, CX * LANES), F32),
            pltpu.VMEM((CY, NP, CX * LANES), F32),
        ],
    )(adj, coef_y, line_order, mats, terms)
    return out.reshape(NP, CX, CY, LANES)


def solution(mesh):
    grid = P(None, "gx", "gy", None)
    in_specs = (grid, grid, grid) + (P(),) * 7 + (P("gy", None), P("gx", None))
    return jax.shard_map(
        per_device, mesh=mesh, in_specs=in_specs, out_specs=grid, check_vma=False
    )
```

profile of v0, /device:TPU:32, one launch (start us, length us, event | category | flops | bytes accessed | tf_op | source)
XLA Modules:
  0.0 98.6 jit_solution(17388886989822972053)
XLA Ops:
  0.0 0.8 bitcast_dynamic-update-slice_fusion.5
  0.9 0.8 bitcast_dynamic-update-slice_fusion.4
  1.6 0.8 bitcast_dynamic-update-slice_fusion.3
  2.4 0.9 constant_dynamic-update-slice_fusion
  3.3 0.8 bitcast_dynamic-update-slice_fusion.2
  4.0 0.8 bitcast_dynamic-update-slice_fusion.1
  4.8 0.8 bitcast_dynamic-update-slice_fusion
  5.6 0.1 copy.13
  5.7 0.3 pad_maximum_fusion.mats_ref
  6.0 0.5 copy-done.1
  6.5 0.2 copy-done.4
  6.7 3.7 %shard_map.118 = f32[8,72,128]{2,1,0:T(8,128)} custom-call(s32[1]{0:T(128)} %bitcast.rank_ref, f32[2048,128]{1,0:T(8,128)S(1)} %bitcast.19, f32[3,32,128]{2,1,0:T(8,128)S(1)} %bitcast.21, s32[4,128]{1,0:T(4,128)S(1)} %copy-done.4, f32[576,256]{1,0:T(8,128)S(1)} %pad_maximum_fusion.mats_ref), custom_call_target="tpu_custom_call" | custom-call | tf_op jit(solution)/shard_map/pallas_call | solution.py:545
  10.4 4.3 %all-to-all-start = ((f32[8,72,128]{2,1,0:T(8,128)}), f32[8,72,128]{2,1,0:T(8,128)S(1)}, u32[]{:S(2)}, u32[]{:S(2)}) async-start(f32[8,72,128]{2,1,0:T(8,128)} %shard_map.118), calls=%async_computation | async-start | bytes 589824 | tf_op jit(solution)/shard_map/all_to_all | solution.py:552
  14.7 3.7 %shard_map.119 = (bf16[704,256]{1,0:T(8,128)(2,1)S(1)}, bf16[3,64,256]{2,1,0:T(8,128)(2,1)S(1)}, bf16[3,64,256]{2,1,0:T(8,128)(2,1)S(1)}, f32[8,128]{1,0:T(8,128)S(1)}) custom-call(f32[576,256]{1,0:T(8,128)S(1)} %pad_maximum_fusion.mats_ref), custom_call_target="tpu_custom_call" | custom-call | tf_op jit(solution)/shard_map/pallas_call | solution.py:513
  18.5 4.2 %all-to-all-done.in_ref = f32[8,72,128]{2,1,0:T(8,128)S(1)} async-done(((f32[8,72,128]{2,1,0:T(8,128)}), f32[8,72,128]{2,1,0:T(8,128)S(1)}, u32[]{:S(2)}, u32[]{:S(2)}) %all-to-all-start) | async-done | bytes 294944 | tf_op jit(solution)/shard_map/all_to_all | solution.py:552
  22.6 1.7 %shard_map.120 = f32[8,64,128]{2,1,0:T(8,128)S(1)} custom-call(f32[8,72,128]{2,1,0:T(8,128)S(1)} %all-to-all-done.in_ref, bf16[704,256]{1,0:T(8,128)(2,1)S(1)} %get-tuple-element.15.gain_ref, bf16[3,64,256]{2,1,0:T(8,128)(2,1)S(1)} %get-tuple-element.16.up_ref, bf16[3,64,256]{2,1,0:T(8,128)(2,1)S(1)} %get-tuple-element.17.down_ref, ...), custom_call_target="tpu_custom_call" | custom-call | tf_op jit(solution)/shard_map/pallas_call | solution.py:554
  24.4 10.1 %all_to_all.20.in_ref = f32[8,64,128]{2,1,0:T(8,128)S(1)} all-to-all(f32[8,64,128]{2,1,0:T(8,128)S(1)} %shard_map.120), channel_id=1, replica_groups=mesh['gx'=8,'gy'=32] {'gx'}, dimensions={0} | all-to-all | bytes 524288 | tf_op jit(solution)/shard_map/all_to_all | solution.py:555
  34.5 5.2 %shard_map.121 = (f32[4,64,1024]{2,1,0:T(8,128)S(1)}, f32[32,40,128]{2,1,0:T(8,128)}) custom-call(s32[1]{0:T(128)} %bitcast.rank_ref, f32[2048,128]{1,0:T(8,128)S(1)} %bitcast.20, f32[3,32,128]{2,1,0:T(8,128)S(1)} %bitcast.22, s32[4,128]{1,0:T(4,128)S(1)} %copy-done.4, f32[576,256]{1,0:T(8,128)S(1)} %pad_maximum_fusion.mats_ref, ...), custom_call_target="tpu_custom_call" | custom-call | tf_op jit(solution)/shard_map/pallas_call | solution.py:557
  39.7 11.4 %all-to-all-start.2 = ((f32[32,40,128]{2,1,0:T(8,128)}), f32[32,40,128]{2,1,0:T(8,128)S(1)}, u32[]{:S(2)}, u32[]{:S(2)}) async-start(f32[32,40,128]{2,1,0:T(8,128)} %get-tuple-element.20), calls=%async_computation.2 | async-start | bytes 1310720 | tf_op jit(solution)/shard_map/all_to_all | solution.py:567
  51.0 2.4 %shard_map.122 = (bf16[256,256]{1,0:T(8,128)(2,1)S(1)}, bf16[5,64,256]{2,1,0:T(8,128)(2,1)S(1)}, bf16[5,64,256]{2,1,0:T(8,128)(2,1)S(1)}, f32[8,128]{1,0:T(8,128)S(1)}) custom-call(f32[576,256]{1,0:T(8,128)S(1)} %pad_maximum_fusion.mats_ref), custom_call_target="tpu_custom_call" | custom-call | tf_op jit(solution)/shard_map/pallas_call | solution.py:513
  53.5 17.5 %all-to-all-done.2.in_ref = f32[32,40,128]{2,1,0:T(8,128)S(1)} async-done(((f32[32,40,128]{2,1,0:T(8,128)}), f32[32,40,128]{2,1,0:T(8,128)S(1)}, u32[]{:S(2)}, u32[]{:S(2)}) %all-to-all-start.2) | async-done | bytes 655392 | tf_op jit(solution)/shard_map/all_to_all | solution.py:567
  71.0 3.1 %shard_map.123 = f32[32,32,128]{2,1,0:T(8,128)S(1)} custom-call(f32[32,40,128]{2,1,0:T(8,128)S(1)} %all-to-all-done.2.in_ref, bf16[256,256]{1,0:T(8,128)(2,1)S(1)} %get-tuple-element.21.gain_ref, bf16[5,64,256]{2,1,0:T(8,128)(2,1)S(1)} %get-tuple-element.22.up_ref, bf16[5,64,256]{2,1,0:T(8,128)(2,1)S(1)} %get-tuple-element.23.down_ref, ...), custom_call_target="tpu_custom_call" | custom-call | tf_op jit(solution)/shard_map/pallas_call | solution.py:568
  74.1 21.6 %all_to_all.21.in_ref = f32[32,32,128]{2,1,0:T(8,128)S(1)} all-to-all(f32[32,32,128]{2,1,0:T(8,128)S(1)} %shard_map.123), channel_id=1, replica_groups=mesh['gx'=8,'gy'=32] {'gy'}, dimensions={0} | all-to-all | bytes 1048576 | tf_op jit(solution)/shard_map/all_to_all | solution.py:571
  95.7 2.9 %shard_map.124 = f32[2048,128]{1,0:T(8,128)} custom-call(f32[4,64,1024]{2,1,0:T(8,128)S(1)} %get-tuple-element.19.adj_ref, f32[3,32,128]{2,1,0:T(8,128)S(1)} %bitcast.24, s32[8,128]{1,0:T(8,128)S(1)} %copy-done.3, f32[576,256]{1,0:T(8,128)S(1)} %pad_maximum_fusion.mats_ref, f32[32,32,128]{2,1,0:T(8,128)S(1)} %all_to_all.21.in_ref), custom_call_target="tpu_custom_call" | custom-call | tf_op jit(solution)/shard_map/pallas_call | solution.py:572
  (8 shorter events, 0.0 us)
Async XLA Ops:
  0.0 6.0 %copy-start = (f32[64,8,4,128]{3,2,1,0:T(4,128)S(1)}, f32[64,8,4,128]{3,2,1,0:T(4,128)}, u32[]{:S(2)}) copy-start(f32[64,8,4,128]{3,2,1,0:T(4,128)} %param.12) | copy-start | bytes 3145732
  5.7 0.8 copy-start.1
  6.0 0.7 copy-start.4
  10.4 12.2 %all-to-all-start = ((f32[8,72,128]{2,1,0:T(8,128)}), f32[8,72,128]{2,1,0:T(8,128)S(1)}, u32[]{:S(2)}, u32[]{:S(2)}) async-start(f32[8,72,128]{2,1,0:T(8,128)} %shard_map.118), calls=%async_computation | async-start | bytes 589824 | tf_op jit(solution)/shard_map/all_to_all | solution.py:552
  24.4 10.1 %copy-start.2 = (f32[3,8,4,128]{3,2,1,0:T(4,128)S(1)}, f32[3,8,4,128]{3,2,1,0:T(4,128)}, u32[]{:S(2)}) copy-start(f32[3,8,4,128]{3,2,1,0:T(4,128)} %param.14) | copy-start | bytes 147460
  24.4 10.1 %copy-start.3 = (s32[8,128]{1,0:T(8,128)S(1)}, s32[8,128]{1,0:T(8,128)}, u32[]{:S(2)}) copy-start(s32[8,128]{1,0:T(8,128)} %order_ref.3) | copy-start | bytes 12292
  39.7 31.3 %all-to-all-start.2 = ((f32[32,40,128]{2,1,0:T(8,128)}), f32[32,40,128]{2,1,0:T(8,128)S(1)}, u32[]{:S(2)}, u32[]{:S(2)}) async-start(f32[32,40,128]{2,1,0:T(8,128)} %get-tuple-element.20), calls=%async_computation.2 | async-start | bytes 1310720 | tf_op jit(solution)/shard_map/all_to_all | solution.py:567
where the time goes:
time: 99.4 us; the launch traced here: 98.6 us
  blocking collectives  31.7 us (32%)
  Pallas kernels  22.8 us (23%)
  waiting for transfers between devices  21.6 us (22%)
  starting transfers between devices  15.7 us (16%)
  local copies, waits for them, and re-layouts  6.39 us (6%)
    all_to_all x1, blocking collectives, per_device(): terms = lax.all_to_all(back, 'gy', 0, 0, tiled=True)  21.6 us
    all_to_all x1, waiting for transfers between devices, per_device(): got = lax.all_to_all(sent, 'gy', 0, 0, tiled=True)  17.5 us
    all_to_all x1, starting transfers between devices, per_device(): got = lax.all_to_all(sent, 'gy', 0, 0, tiled=True)  11.4 us
    all_to_all x1, blocking collectives, per_device(): terms = lax.all_to_all(back, 'gx', 0, 0, tiled=True)  10.1 us
    pallas_call x2, Pallas kernels, prepared(): return call(kernel, outs, 1)(mats)  6.17 us
    unnamed x16, local copies, waits for them, and re-layouts  5.48 us
    pallas_call x1, Pallas kernels, per_device(): call(middle_kernel, (shape(CY, NP, CX * LANES), shape(SY, 40, LANES)), 7,...  5.18 us
    all_to_all x1, starting transfers between devices, per_device(): got = lax.all_to_all(sent, 'gx', 0, 0, tiled=True)  4.3 us
  transfers between devices with their start and end apart: 2, of which 2 were waited for; matrix products, arithmetic and copies ran while one was open for 0% of the time, Pallas kernels for 6%

commit v1 on v0

v1 whole, which is shorter than its diff:
```python
import jax
import jax.numpy as jnp
from jax import lax
from jax.experimental import pallas as pl
from jax.experimental.pallas import tpu as pltpu
from jax.sharding import PartitionSpec as P

NP = 64
LANES = 128
CX = 8
PIECES = 4
CY = 4
SX = 8
SY = 32
ROWS = 34
F32 = jnp.float32
BF16 = jnp.bfloat16
VMEM_LIMIT = 48 * 1024 * 1024


def rounded(v):
    return v.astype(BF16).astype(F32)


def split_matrix(m):
    high = rounded(m)
    rest = m - high
    mid = rounded(rest)
    low = rest - mid
    part = lax.broadcasted_iota(jnp.int32, m.shape, 1) // NP
    return jnp.where(part == 1, mid, jnp.where(part == 3, low, high)).astype(BF16)


def split_vectors(v):
    high = v.astype(BF16)
    low = (v - high.astype(F32)).astype(BF16)
    return jnp.concatenate([high, high, low, high], axis=0)


def product(parts, vectors):
    return jnp.dot(parts, vectors, preferred_element_type=F32)


def apply(parts, v):
    return product(parts, split_vectors(v))


def lane_iota(shape):
    return lax.broadcasted_iota(jnp.int32, shape, len(shape) - 1)


def roll(v, shift):
    shift = shift % LANES
    return v if shift == 0 else pltpu.roll(v, shift, 1)


def row_of(block):
    return jnp.concatenate([block[r : r + 1] for r in range(block.shape[0])], axis=1)


def columns(v):
    return [v[:, LANES * j : LANES * (j + 1)] for j in range(v.shape[1] // LANES)]


def regroup(blocks, width):
    n = LANES // width
    rolled = [[roll(b, width * k) for k in range(n)] for b in blocks]
    group = lane_iota(blocks[0].shape) // width
    outs = []
    for a in range(n):
        acc = rolled[0][(0 - a) % n]
        for q in range(1, n):
            acc = jnp.where(group == q, rolled[q][(q - a) % n], acc)
        outs.append(acc)
    return outs


def replicate(block, width):
    return regroup([block] * (LANES // width), width)


def shifted(v, t, width, ncol, reverse):
    cols = columns(v)
    group = lane_iota(cols[0].shape) // width
    n = LANES // width
    out = []
    for j in range(ncol):
        k = j + t if reverse else j - t
        carry = abs(k // ncol)
        src = cols[k % ncol]
        if carry:
            if reverse:
                src = jnp.where(group < n - carry, roll(src, -width * carry), 0.0)
            else:
                src = jnp.where(group >= carry, roll(src, width * carry), 0.0)
        out.append(src)
    return jnp.concatenate(out, axis=1)


def scan_segments(v, rate, powers, width, ncol, reverse):
    for k in range(powers.shape[0]):
        t = 1 << k
        v = v + rate * apply(powers[k], shifted(v, t, width, ncol, reverse))
        if k + 1 < powers.shape[0]:
            rate = rate * shifted(rate, t, width, ncol, reverse)
    return v


def tiled(m):
    pair = jnp.concatenate([m, m], axis=0).T
    return jnp.concatenate([pair, pair], axis=1)


def multiply(a, b):
    parts = split_matrix(a)
    high = b.astype(BF16)
    rest = b - high.astype(F32)
    mid = rest.astype(BF16)
    low = (rest - mid.astype(F32)).astype(BF16)
    none = jnp.zeros_like(low)
    return product(parts, jnp.concatenate([high, high, mid, high], axis=0)) + product(
        parts, jnp.concatenate([low, mid, none, none], axis=0)
    )


def prepare(cells, doublings, up, down, scale, bounds, gain_ref, from_ref, up_ref, down_ref, norm_ref):
    halves = cells.bit_length() - 1
    ups, downs = [up], [down]
    for _ in range(halves):
        ups.append(multiply(ups[-1], ups[-1]))
        downs.append(multiply(downs[-1], downs[-1]))
    scaled = scale
    stack = down
    for k in range(halves):
        scaled = jnp.concatenate([scaled, multiply(scaled, ups[k])], axis=0)
        stack = jnp.concatenate([stack, multiply(stack, downs[k])], axis=0)
    from_ref[0 : cells * NP, :] = split_matrix(scaled)
    for j in range(cells):
        rows = slice(NP * j, NP * (j + 1))
        gain_ref[rows, :] = split_matrix(multiply(stack[rows], scaled[rows]))
    if bounds is not None:
        for k in range(halves):
            bounds = multiply(bounds, ups[k])
        from_ref[cells * NP :, :] = split_matrix(bounds)
        for kind in range(3):
            rows = slice(NP * (cells + kind), NP * (cells + kind + 1))
            ends = bounds[NP * kind : NP * (kind + 1)]
            gain_ref[rows, :] = split_matrix(multiply(downs[halves], ends))
    norm_ref[...] = jnp.zeros(norm_ref.shape, F32)
    for row, (power, ref) in enumerate(((ups[halves], up_ref), (downs[halves], down_ref))):
        norm = jnp.max(jnp.sum(jnp.abs(power[:, :NP]), axis=1, keepdims=True), axis=0, keepdims=True)
        norm = jnp.maximum(norm, 1e-30)
        norm_ref[row : row + 1, :] = jnp.broadcast_to(norm, (1, LANES))
        power = power / norm
        for k in range(doublings):
            ref[k] = split_matrix(power)
            if k + 1 < doublings:
                power = multiply(power, power)


def prepare_kernel(mats_ref, raw_ref, parts_ref, *outs):
    ux, wx, b0, b1, b2, dx = [mats_ref[NP * k : NP * (k + 1), :] for k in range(6)]
    uy, wy, dy = [tiled(raw_ref[k]) for k in range(3)]
    for k, m in enumerate((dx, uy, wy, dy)):
        parts_ref[NP * k : NP * (k + 1), :] = split_matrix(m)
    prepare(CX, 3, ux, dx, wx, jnp.concatenate([b0, b1, b2], axis=0), *outs[:5])
    prepare(CY, 5, uy, dy, wy, None, *outs[5:])


def x_rates(coef_ref, which, i):
    return coef_ref[which, CY * i : CY * (i + 1), :]


def x_local_kernel(
    rank_ref,
    rhs_hbm,
    coef_hbm,
    flags_hbm,
    ux,
    wx,
    dx,
    b,
    uy,
    wy,
    dy,
    coef_y_hbm,
    order_hbm,
    out_ref,
    scaled_ref,
    mats_ref,
    raw_y_ref,
    coef_ref,
    flags_ref,
    coef_y_ref,
    order_ref,
    rhs_ref,
    raw_ref,
    bounds_ref,
    sems,
):
    rank = rank_ref[0]
    sources = [ux, wx, b, dx, coef_hbm, flags_hbm]
    targets = [raw_ref.at[0], raw_ref.at[1], bounds_ref, raw_ref.at[2], coef_ref, flags_ref]
    for k in range(PIECES):
        sources.append(rhs_hbm.at[:, 8 * k : 8 * (k + 1), :])
        targets.append(rhs_ref.at[k])
    sources += [uy, wy, dy, coef_y_hbm, order_hbm]
    targets += [raw_y_ref.at[0], raw_y_ref.at[1], raw_y_ref.at[2], coef_y_ref, order_ref]
    copies = []
    for k, (source, target) in enumerate(zip(sources, targets)):
        copies.append(pltpu.make_async_copy(source, target, sems.at[k]))
        copies[-1].start()
    for copy in copies[:6]:
        copy.wait()

    def place(row, m):
        value = tiled(m)
        mats_ref[NP * row : NP * (row + 1), :] = value
        return split_matrix(value)

    every = jnp.concatenate(
        [place(0, raw_ref[0]), place(1, raw_ref[1])] + [place(2 + k, bounds_ref[k]) for k in range(3)],
        axis=0,
    )
    both = every[: 2 * NP]
    down = place(5, raw_ref[2])
    planes = rhs_ref.reshape(PIECES * NP * 8, LANES)

    flags = row_of(flags_ref[...])
    carry = 0.0
    for i in range(CX):
        k = CY * i // 8
        if CY * i % 8 == 0:
            copies[6 + k].wait()
        start = k * NP * 8 + CY * i % 8
        f = carry + jnp.concatenate(
            [planes[pl.ds(start + y, NP, stride=8), :] for y in range(CY)], axis=1
        )
        if i == 0 or i == CX - 1:
            out = apply(every, f)
            ends = out[2 * NP :]
            chosen = jnp.where(
                flags == 0, ends[:NP], jnp.where(flags == 1, ends[NP : 2 * NP], ends[2 * NP :])
            )
            scaled = jnp.where(rank == (0 if i == 0 else SX - 1), chosen, out[NP : 2 * NP])
        else:
            out = apply(both, f)
            scaled = out[NP:]
        carry = row_of(x_rates(coef_ref, 1, i)) * out[:NP]
        scaled_ref[i] = scaled * row_of(1.0 / x_rates(coef_ref, 2, i))
    f = carry
    carry = 0.0
    for i in reversed(range(CX)):
        carry = row_of(x_rates(coef_ref, 0, i)) * apply(down, scaled_ref[i] + carry)
    g = carry
    for copy in copies[6 + PIECES :]:
        copy.wait()
    for y, (fy, gy) in enumerate(zip(columns(f), columns(g))):
        even, odd = regroup([fy, gy], NP)
        out_ref[2 * y, 0:NP, :] = even
        out_ref[2 * y + 1, 0:NP, :] = odd
    down_rate = x_rates(coef_ref, 0, 0)
    up_rate = jnp.ones_like(down_rate)
    gains = []
    for i in range(CX):
        gains.append(down_rate * up_rate / x_rates(coef_ref, 2, i))
        up_rate = up_rate * x_rates(coef_ref, 1, i)
        if i + 1 < CX:
            down_rate = down_rate * x_rates(coef_ref, 0, i + 1)
    last = gains.pop()
    is_last = rank == SX - 1
    flags = flags_ref[...]
    gains.append(jnp.where(is_last, 0.0, last))
    for kind in range(3):
        gains.append(jnp.where(jnp.logical_and(is_last, flags == kind), last, 0.0))
    values = [up_rate, down_rate] + gains + [jnp.zeros_like(last)] * 3
    for r in range(8):
        even, odd = regroup([values[2 * r], values[2 * r + 1]], NP)
        for y in range(CY):
            out_ref[2 * y, NP + r : NP + r + 1, :] = even[y : y + 1]
            out_ref[2 * y + 1, NP + r : NP + r + 1, :] = odd[y : y + 1]


def x_owner_kernel(in_ref, gain_ref, up_ref, down_ref, norm_ref, out_ref):
    half = SX // 2
    fs, gs, sa, sb = [], [], [], []
    for j in range(half):
        f, g = regroup([in_ref[j], in_ref[half + j]], NP)
        fs.append(f[:NP])
        gs.append(g[:NP])
        sa.append(f[NP:])
        sb.append(g[NP:])
    f = jnp.concatenate(fs, axis=1)
    g = jnp.concatenate(gs, axis=1)
    even = jnp.concatenate(sa, axis=1)
    odd = jnp.concatenate(sb, axis=1)
    scalar = [(even if k % 2 == 0 else odd)[k // 2 : k // 2 + 1] for k in range(13)]
    width, ncol = NP, half
    up_rate = scalar[0] * norm_ref[0:1, 0:1]
    down_rate = scalar[1] * norm_ref[1:2, 0:1]
    h = scan_segments(
        shifted(f, 1, width, ncol, False),
        shifted(up_rate, 1, width, ncol, False),
        up_ref,
        width,
        ncol,
        False,
    )
    vectors = split_vectors(h)
    through = product(gain_ref[0 : CX * NP], vectors)
    for i in range(CX):
        g = g + scalar[2 + i] * through[NP * i : NP * (i + 1)]
    ends = product(gain_ref[CX * NP :], vectors[:, LANES * (half - 1) :])
    extra = 0.0
    for kind in range(3):
        extra = extra + (
            scalar[10 + kind][:, LANES * (half - 1) :] * ends[NP * kind : NP * (kind + 1)]
        )
    g = jnp.concatenate([g[:, : LANES * (half - 1)], g[:, LANES * (half - 1) :] + extra], axis=1)
    e = scan_segments(
        shifted(g, 1, width, ncol, True),
        shifted(down_rate, 1, width, ncol, True),
        down_ref,
        width,
        ncol,
        True,
    )
    for j, (hj, ej) in enumerate(zip(columns(h), columns(e))):
        first, second = regroup([hj, ej], NP)
        out_ref[j] = first
        out_ref[half + j] = second


def y_rates(coef_ref, which, flip, p):
    here = coef_ref[which, pl.ds(p, CX, stride=CY), :]
    there = coef_ref[which, pl.ds(CY - 1 - p, CX, stride=CY), :]
    return jnp.where(flip, there, here)


def middle_kernel(
    rank_ref,
    local_ref,
    coef_ref,
    flags_ref,
    parts_ref,
    from_ref,
    in_ref,
    coef_y_ref,
    order_ref,
    scaled_ref,
    out_ref,
    adj_ref,
):
    rank = rank_ref[0]
    parts = parts_ref[...]
    down, both_y, down_y = parts[:NP], parts[NP : 3 * NP], parts[3 * NP :]
    hs, es = [], []
    for y in range(CY):
        h, e = regroup([in_ref[2 * y], in_ref[2 * y + 1]], NP)
        hs.append(h)
        es.append(e)
    through = apply(from_ref[...], jnp.concatenate(hs, axis=1))
    flags = row_of(flags_ref[...])
    up_rates = [jnp.ones((CY, LANES), F32)]
    for i in range(CX - 1):
        up_rates.append(up_rates[-1] * x_rates(coef_ref, 1, i))
    carry = jnp.concatenate(es, axis=1)
    for i in reversed(range(CX)):
        term = through[NP * i : NP * (i + 1)]
        if i == CX - 1:
            ends = through[NP * CX :]
            chosen = jnp.where(
                flags == 0, ends[:NP], jnp.where(flags == 1, ends[NP : 2 * NP], ends[2 * NP :])
            )
            term = jnp.where(rank == SX - 1, chosen, term)
        g = local_ref[i] + row_of(up_rates[i] / x_rates(coef_ref, 2, i)) * term + carry
        for y in range(CY):
            adj_ref[y, :, LANES * i : LANES * (i + 1)] = g[:, LANES * y : LANES * (y + 1)]
        if i > 0:
            carry = row_of(x_rates(coef_ref, 0, i)) * apply(down, g)

    flip = order_ref[...] > 0
    flip_row = row_of(order_ref[...]) > 0

    def oriented(which, p):
        return y_rates(coef_y_ref, which, flip, p)

    carry = 0.0
    for p in range(CY):
        out = apply(both_y, jnp.where(flip_row, adj_ref[CY - 1 - p], adj_ref[p]) + carry)
        carry = row_of(oriented(1, p)) * out[:NP]
        scaled_ref[p] = out[NP:] * row_of(1.0 / oriented(2, p))
    f = carry
    carry = 0.0
    for p in reversed(range(CY)):
        carry = row_of(oriented(0, p)) * apply(down_y, scaled_ref[p] + carry)
    g = carry

    down_rate = oriented(0, 0)
    up_rate = jnp.ones_like(down_rate)
    gains = []
    for p in range(CY):
        gains.append(down_rate * up_rate / oriented(2, p))
        up_rate = up_rate * oriented(1, p)
        if p + 1 < CY:
            down_rate = down_rate * oriented(0, p + 1)
    first = regroup([up_rate, down_rate, gains[0], gains[1]], 32)
    second = regroup([gains[2], gains[3], flip.astype(F32), jnp.zeros_like(up_rate)], 32)
    for x, (fx, gx) in enumerate(zip(columns(f), columns(g))):
        chunks = regroup([fx[:32], fx[32:], gx[:32], gx[32:]], 32)
        for a in range(4):
            row = ROWS * (4 * x + a)
            out_ref[row : row + 32, :] = chunks[a]
            out_ref[row + 32 : row + 33, :] = first[a][x : x + 1]
            out_ref[row + 33 : row + 34, :] = second[a][x : x + 1]


def y_owner_kernel(in_ref, gain_ref, up_ref, down_ref, norm_ref, out_ref, res_ref):
    width, ncol = 32, 8
    flip = replicate(in_ref[33:34, :], width)[2] > 0.5

    def oriented(s):
        t = SY - 1 - s
        return jnp.where(flip, in_ref[ROWS * t : ROWS * (t + 1), :], in_ref[ROWS * s : ROWS * (s + 1), :])

    fs, gs, ss = [], [], []
    for j in range(ncol):
        outs = regroup([oriented(ncol * a + j) for a in range(4)], width)
        fs.append(jnp.concatenate([outs[0][:32], outs[1][:32]], axis=0))
        gs.append(jnp.concatenate([outs[2][:32], outs[3][:32]], axis=0))
        ss.append([o[32:33] for o in outs] + [o[33:34] for o in outs[:2]])
    f = jnp.concatenate(fs, axis=1)
    g = jnp.concatenate(gs, axis=1)
    scalars = [jnp.concatenate([s[k] for s in ss], axis=1) for k in range(6)]
    up_rate = scalars[0] * norm_ref[0:1, 0:1]
    down_rate = scalars[1] * norm_ref[1:2, 0:1]
    h = scan_segments(
        shifted(f, 1, width, ncol, False),
        shifted(up_rate, 1, width, ncol, False),
        up_ref,
        width,
        ncol,
        False,
    )
    through = apply(gain_ref[...], h)
    for p in range(CY):
        g = g + scalars[2 + p] * through[NP * p : NP * (p + 1)]
    e = scan_segments(
        shifted(g, 1, width, ncol, True),
        shifted(down_rate, 1, width, ncol, True),
        down_ref,
        width,
        ncol,
        True,
    )
    for j, (hj, ej) in enumerate(zip(columns(h), columns(e))):
        outs = regroup([hj[:32], hj[32:], ej[:32], ej[32:]], width)
        for a in range(4):
            res_ref[ncol * a + j] = outs[a]
    for s in range(SY):
        out_ref[s] = jnp.where(flip, res_ref[SY - 1 - s], res_ref[s])


def y_final_kernel(local_ref, coef_y_ref, order_ref, parts_ref, from_ref, in_ref, out_ref, solved_ref):
    down = parts_ref[3 * NP :, :]
    flip = order_ref[...] > 0
    flip_row = row_of(order_ref[...]) > 0

    def oriented(which, p):
        return y_rates(coef_y_ref, which, flip, p)

    hs, es = [], []
    for x in range(CX):
        outs = regroup([in_ref[4 * x + a] for a in range(4)], 32)
        hs.append(jnp.concatenate(outs[:2], axis=0))
        es.append(jnp.concatenate(outs[2:], axis=0))
    through = apply(from_ref[...], jnp.concatenate(hs, axis=1))
    up_rates = [jnp.ones((CX, LANES), F32)]
    for p in range(CY - 1):
        up_rates.append(up_rates[-1] * oriented(1, p))
    carry = jnp.concatenate(es, axis=1)
    for p in reversed(range(CY)):
        term = row_of(up_rates[p] / oriented(2, p)) * through[NP * p : NP * (p + 1)]
        g = local_ref[p] + term + carry
        solved_ref[p] = g
        if p > 0:
            carry = row_of(oriented(0, p)) * apply(down, g)
    for y in range(CY):
        plane = jnp.where(flip_row, solved_ref[CY - 1 - y], solved_ref[y])
        for x, block in enumerate(columns(plane)):
            out_ref[pl.ds(CY * x + y, NP, stride=CX * CY), :] = block


def in_hbm(a):
    return pltpu.with_memory_space_constraint(a, pltpu.HBM)


def shape(*dims, dtype=F32):
    return jax.ShapeDtypeStruct(dims, dtype)


def call(kernel, out_shape, n_in, scratch=(), scalars=0, space=pltpu.VMEM):
    whole = pl.BlockSpec(memory_space=pltpu.VMEM)
    specs = [pl.BlockSpec(memory_space=pltpu.SMEM)] * scalars
    specs += [pl.BlockSpec(memory_space=space)] * n_in
    outs = jax.tree.map(lambda _: whole, out_shape)
    return pl.pallas_call(
        kernel,
        out_shape=out_shape,
        in_specs=specs,
        out_specs=outs,
        scratch_shapes=list(scratch),
        compiler_params=pltpu.CompilerParams(vmem_limit_bytes=VMEM_LIMIT),
    )


def prepared_shapes(cells, extra, doublings):
    return (
        shape((cells + extra) * NP, 4 * NP, dtype=BF16),
        shape((cells + extra) * NP, 4 * NP, dtype=BF16),
        shape(doublings, NP, 4 * NP, dtype=BF16),
        shape(doublings, NP, 4 * NP, dtype=BF16),
        shape(8, LANES),
    )


def per_device(
    rhs,
    coef_x,
    coef_y,
    out_coupling_x,
    in_coupling_x,
    inverse_x,
    boundary_inverse,
    out_coupling_y,
    in_coupling_y,
    inverse_y,
    bc_flags,
    line_order,
):
    rank = lax.axis_index("gx").astype(jnp.int32).reshape(1)
    mats = (
        out_coupling_x,
        inverse_x,
        in_coupling_x,
        boundary_inverse,
        out_coupling_y,
        inverse_y,
        in_coupling_y,
    )
    rhs = rhs.reshape(NP, CX * CY, LANES)
    coef_x = coef_x.reshape(3, CX * CY, LANES)
    coef_y = coef_y.reshape(3, CX * CY, LANES)

    sent, local, tiles, raw_y, coef_x, flags, coef_y, order = call(
        x_local_kernel,
        (
            shape(SX, NP + 8, LANES),
            shape(CX, NP, CY * LANES),
            shape(6 * NP, 4 * NP),
            shape(3, NP, NP),
            shape(3, CX * CY, LANES),
            shape(CY, LANES, dtype=jnp.int32),
            shape(3, CX * CY, LANES),
            shape(CX, LANES, dtype=jnp.int32),
        ),
        12,
        [
            pltpu.VMEM((PIECES, NP, 8, LANES), F32),
            pltpu.VMEM((3, NP, NP), F32),
            pltpu.VMEM((3, NP, NP), F32),
            pltpu.SemaphoreType.DMA((11 + PIECES,)),
        ],
        1,
        pltpu.HBM,
    )(rank, *[in_hbm(a) for a in (rhs, coef_x, bc_flags) + mats + (coef_y, line_order)])
    got = lax.all_to_all(sent, "gx", 0, 0, tiled=True)
    prep_shapes = (shape(4 * NP, 4 * NP, dtype=BF16),)
    prep_shapes += prepared_shapes(CX, 3, 3) + prepared_shapes(CY, 0, 5)
    prep = call(prepare_kernel, prep_shapes, 2)(tiles, raw_y)
    parts, gain_x, from_x, up_x, down_x, norm_x, gain_y, from_y, up_y, down_y, norm_y = prep
    back = call(x_owner_kernel, shape(SX, NP, LANES), 5)(got, gain_x, up_x, down_x, norm_x)
    terms = lax.all_to_all(back, "gx", 0, 0, tiled=True)
    local, sent = call(
        middle_kernel,
        (shape(CY, NP, CX * LANES), shape(SY * ROWS, LANES)),
        8,
        [pltpu.VMEM((CY, NP, CX * LANES), F32)],
        1,
    )(rank, local, coef_x, flags, parts, from_x, terms, coef_y, order)
    got = lax.all_to_all(sent.reshape(SY, ROWS // 2, 2, LANES), "gy", 0, 0, tiled=True)
    back = call(
        y_owner_kernel, shape(SY, 32, LANES), 5, [pltpu.VMEM((SY, 32, LANES), F32)]
    )(got.reshape(SY * ROWS, LANES), gain_y, up_y, down_y, norm_y)
    terms = lax.all_to_all(back, "gy", 0, 0, tiled=True)
    out = call(
        y_final_kernel,
        shape(NP * CX * CY, LANES),
        6,
        [pltpu.VMEM((CY, NP, CX * LANES), F32)],
    )(local, coef_y, order, parts, from_y, terms)
    return out.reshape(NP, CX, CY, LANES)


def solution(mesh):
    grid = P(None, "gx", "gy", None)
    in_specs = (grid, grid, grid) + (P(),) * 7 + (P("gy", None), P("gx", None))
    return jax.shard_map(
        per_device, mesh=mesh, in_specs=in_specs, out_specs=grid, check_vma=False
    )
```

time: 99.4 us -> 89.5 us (0.900)
  blocking collectives: 31.7 us -> 60.7 us
  waiting for transfers between devices: 21.6 us -> 4.06 us
  starting transfers between devices: 15.7 us -> 4.3 us
  local copies, waits for them, and re-layouts: 6.39 us -> 0.61 us
  Pallas kernels: 22.8 us -> 19.4 us
    all_to_all x0 -> x1, blocking collectives: none -> 29.1 us  [per_device(): lax.all_to_all(sent.reshape(SY, ROWS // 2, 2, LANES), 'gy', 0, 0, tiled=T...]
    all_to_all x1 -> x0, waiting for transfers between devices: 17.5 us -> none  [per_device(): got = lax.all_to_all(sent, 'gy', 0, 0, tiled=True)]
    all_to_all x1 -> x0, starting transfers between devices: 11.4 us -> none  [per_device(): got = lax.all_to_all(sent, 'gy', 0, 0, tiled=True)]
    unnamed x16 -> x4, local copies, waits for them, and re-layouts: 5.48 us -> 0.61 us
    pallas_call x6 -> x5, Pallas kernels: 19.7 us -> 16.2 us  [the longest x1 5.02 us: per_device(): call(x_local_kernel, (shape(SX, NP + 8, LANES), shape(CX, NP, CY * LANES)...]
  transfers between devices with their start and end apart: 2 -> 1, of which waited for: 2 -> 1; matrix products, arithmetic and copies ran while one was open for 0% -> 0% of each run, Pallas kernels for 6% -> 4%
where the time goes in v1:
time: 89.5 us; the launch traced here: 89.2 us
  blocking collectives  60.7 us (68%)
  Pallas kernels  19.4 us (22%)
  starting transfers between devices  4.3 us (5%)
  waiting for transfers between devices  4.06 us (5%)
    all_to_all x1, blocking collectives, per_device(): lax.all_to_all(sent.reshape(SY, ROWS // 2, 2, LANES), 'gy', 0, 0, tiled=T...  29.1 us
    all_to_all x1, blocking collectives, per_device(): terms = lax.all_to_all(back, 'gy', 0, 0, tiled=True)  21.6 us
    all_to_all x1, blocking collectives, per_device(): terms = lax.all_to_all(back, 'gx', 0, 0, tiled=True)  10.1 us
    pallas_call x1, Pallas kernels, per_device(): call(x_local_kernel, (shape(SX, NP + 8, LANES), shape(CX, NP, CY * LANES)...  5.02 us
    all_to_all x1, starting transfers between devices, per_device(): got = lax.all_to_all(sent, 'gx', 0, 0, tiled=True)  4.3 us
    all_to_all x1, waiting for transfers between devices, per_device(): got = lax.all_to_all(sent, 'gx', 0, 0, tiled=True)  4.06 us
    pallas_call x1, Pallas kernels, per_device(): prep = call(prepare_kernel, prep_shapes, 2)(tiles, raw_y)  3.83 us
    pallas_call x1, Pallas kernels, per_device(): call(y_owner_kernel, shape(SY, 32, LANES), 5, [pltpu.VMEM((SY, 32, LANES)...  3.19 us
  transfers between devices with their start and end apart: 1, of which 1 were waited for; matrix products, arithmetic and copies ran while one was open for 0% of the time, Pallas kernels for 4%

profile of v1, /device:TPU:32, one launch (start us, length us, event | category | flops | bytes accessed | tf_op | source)
XLA Modules:
  0.0 89.2 jit_solution(3592159652941343909)
XLA Ops:
  0.0 5.0 %shard_map.118 = (f32[8,72,128]{2,1,0:T(8,128)}, f32[8,64,512]{2,1,0:T(8,128)S(1)}, f32[384,256]{1,0:T(8,128)S(1)}, f32[3,64,64]{2,1,0:T(8,128)S(1)}, f32[3,32,1...) custom-call(s32[1]{0:T(128)} %bitcast.rank_ref, ...), custom_call_target="tpu_custom_call" | custom-call | tf_op jit(solution)/shard_map/pallas_call | solution.py:555
  5.0 0.0 copy-start
  5.0 0.6 copy-done
  5.6 4.3 %all-to-all-start = ((f32[8,72,128]{2,1,0:T(8,128)}), f32[8,72,128]{2,1,0:T(8,128)S(1)}, u32[]{:S(2)}, u32[]{:S(2)}) async-start(f32[8,72,128]{2,1,0:T(8,128)} %get-tuple-element.33), calls=%async_computation | async-start | bytes 589824 | tf_op jit(solution)/shard_map/all_to_all | solution.py:577
  9.9 3.8 %shard_map.119 = (bf16[256,256]{1,0:T(8,128)(2,1)S(1)}, bf16[704,256]{1,0:T(8,128)(2,1)S(1)}, bf16[704,256]{1,0:T(8,128)(2,1)S(1)}, bf16[3,64,256]{2,1,0:T(8,128...) custom-call(f32[384,256]{1,0:T(8,128)S(1)} %get-tuple-element.29.mat, ...), custom_call_target="tpu_custom_call" | custom-call | tf_op jit(solution)/shard_map/pallas_call | solution.py:580
  13.8 4.1 %all-to-all-done.in_ref = f32[8,72,128]{2,1,0:T(8,128)S(1)} async-done(((f32[8,72,128]{2,1,0:T(8,128)}), f32[8,72,128]{2,1,0:T(8,128)S(1)}, u32[]{:S(2)}, u32[]{:S(2)}) %all-to-all-start) | async-done | bytes 294944 | tf_op jit(solution)/shard_map/all_to_all | solution.py:577
  17.8 1.7 %shard_map.120 = f32[8,64,128]{2,1,0:T(8,128)S(1)} custom-call(f32[8,72,128]{2,1,0:T(8,128)S(1)} %all-to-all-done.in_ref, bf16[704,256]{1,0:T(8,128)(2,1)S(1)} %get-tuple-element.34.gain_ref, bf16[3,64,256]{2,1,0:T(8,128)(2,1)S(1)} %get-tuple-element.35.up_ref, bf16[3,64,256]{2,1,0:T(8,128)(2,1)S(1)} %get-tuple-element.36.down_ref, ...), custom_call_target="tpu_custom_call" | custom-call | tf_op jit(solution)/shard_map/pallas_call | solution.py:582
  19.6 0.0 copy-start.1
  19.6 10.1 %all_to_all.20.in_ref = f32[8,64,128]{2,1,0:T(8,128)S(1)} all-to-all(f32[8,64,128]{2,1,0:T(8,128)S(1)} %shard_map.120), channel_id=1, replica_groups=mesh['gx'=8,'gy'=32] {'gx'}, dimensions={0} | all-to-all | bytes 524288 | tf_op jit(solution)/shard_map/all_to_all | solution.py:583
  29.7 0.0 copy-done.1
  29.7 3.2 %shard_map.121 = (f32[4,64,1024]{2,1,0:T(8,128)S(1)}, f32[1088,128]{1,0:T(8,128)S(1)}) custom-call(s32[1]{0:T(128)} %bitcast.rank_ref, f32[8,64,512]{2,1,0:T(8,128)S(1)} %get-tuple-element.26.local_ref, f32[3,32,128]{2,1,0:T(8,128)S(1)} %copy-done.1, s32[4,128]{1,0:T(4,128)S(1)} %get-tuple-element.28.flags_ref, ...), custom_call_target="tpu_custom_call" | custom-call | tf_op jit(solution)/shard_map/pallas_call | solution.py:584
  32.9 29.1 %all_to_all.21 = f32[32,17,2,128]{3,2,1,0:T(2,128)S(1)} all-to-all(f32[32,17,2,128]{3,2,1,0:T(2,128)S(1)} %bitcast.8), channel_id=1, replica_groups=mesh['gx'=8,'gy'=32] {'gy'}, dimensions={0} | all-to-all | bytes 1114112 | tf_op jit(solution)/shard_map/all_to_all | solution.py:591
  61.9 3.2 %shard_map.122 = f32[32,32,128]{2,1,0:T(8,128)S(1)} custom-call(f32[1088,128]{1,0:T(8,128)S(1)} %bitcast.7, bf16[256,256]{1,0:T(8,128)(2,1)S(1)} %get-tuple-element.43.gain_ref, bf16[5,64,256]{2,1,0:T(8,128)(2,1)S(1)} %get-tuple-element.44.up_ref, bf16[5,64,256]{2,1,0:T(8,128)(2,1)S(1)} %get-tuple-element.45.down_ref, f32[8,128]{1,0:T(8,128)S(1)} %get-tuple-element.46.norm_ref), custom_call_target="tpu_custom_call" | custom-call | tf_op jit(solution)/shard_map/pallas_call | solution.py:592
  65.1 21.6 %all_to_all.22.in_ref = f32[32,32,128]{2,1,0:T(8,128)S(1)} all-to-all(f32[32,32,128]{2,1,0:T(8,128)S(1)} %shard_map.122), channel_id=1, replica_groups=mesh['gx'=8,'gy'=32] {'gy'}, dimensions={0} | all-to-all | bytes 1048576 | tf_op jit(solution)/shard_map/all_to_all | solution.py:595
  86.7 2.5 %shard_map.123 = f32[2048,128]{1,0:T(8,128)} custom-call(f32[4,64,1024]{2,1,0:T(8,128)S(1)} %get-tuple-element.40.local_ref, f32[3,32,128]{2,1,0:T(8,128)S(1)} %get-tuple-element.38.coef_y_ref, s32[8,128]{1,0:T(8,128)S(1)} %get-tuple-element.39.order_ref, bf16[256,256]{1,0:T(8,128)(2,1)S(1)} %get-tuple-element.31.parts_ref, ...), custom_call_target="tpu_custom_call" | custom-call | tf_op jit(solution)/shard_map/pallas_call | solution.py:596
Async XLA Ops:
  5.0 0.6 copy-start
  5.6 12.2 %all-to-all-start = ((f32[8,72,128]{2,1,0:T(8,128)}), f32[8,72,128]{2,1,0:T(8,128)S(1)}, u32[]{:S(2)}, u32[]{:S(2)}) async-start(f32[8,72,128]{2,1,0:T(8,128)} %get-tuple-element.33), calls=%async_computation | async-start | bytes 589824 | tf_op jit(solution)/shard_map/all_to_all | solution.py:577
  19.6 10.1 %copy-start.1 = (f32[3,32,128]{2,1,0:T(8,128)S(1)}, f32[3,32,128]{2,1,0:T(8,128)}, u32[]{:S(2)}) copy-start(f32[3,32,128]{2,1,0:T(8,128)} %copy-done) | copy-start | bytes 147460

commit v2 on v1

--- a/solution.py
+++ b/solution.py
@@ -97,12 +97,21 @@
     return jnp.concatenate(out, axis=1)
 
 
-def scan_segments(v, rate, powers, width, ncol, reverse):
-    for k in range(powers.shape[0]):
-        t = 1 << k
-        v = v + rate * apply(powers[k], shifted(v, t, width, ncol, reverse))
-        if k + 1 < powers.shape[0]:
-            rate = rate * shifted(rate, t, width, ncol, reverse)
+def block(stack, k):
+    return stack[NP * k : NP * (k + 1)]
+
+
+def scan_segments(v, rate, powers, counts, width, ncol, reverse):
+    stride, row = 1, 0
+    for count in counts:
+        out = apply(powers[NP * row : NP * (row + count), :], v)
+        weight = rate
+        for t in range(1, count + 1):
+            v = v + weight * shifted(block(out, t - 1), stride * t, width, ncol, reverse)
+            weight = rate * shifted(weight, stride, width, ncol, reverse)
+        rate = weight
+        row += count
+        stride *= count + 1
     return v
 
 
@@ -123,7 +132,16 @@
     )
 
 
-def prepare(cells, doublings, up, down, scale, bounds, gain_ref, from_ref, up_ref, down_ref, norm_ref):
+def powers_of(m, count):
+    stack = m
+    while stack.shape[0] < count * NP:
+        done = stack.shape[0] // NP
+        more = min(done, count - done)
+        stack = jnp.concatenate([stack, multiply(stack[: NP * more], block(stack, done - 1))], axis=0)
+    return stack
+
+
+def prepare(cells, far, up, down, scale, bounds, gain_ref, from_ref, up_ref, down_ref, norm_ref):
     halves = cells.bit_length() - 1
     ups, downs = [up], [down]
     for _ in range(halves):
@@ -152,19 +170,29 @@
         norm = jnp.maximum(norm, 1e-30)
         norm_ref[row : row + 1, :] = jnp.broadcast_to(norm, (1, LANES))
         power = power / norm
-        for k in range(doublings):
-            ref[k] = split_matrix(power)
-            if k + 1 < doublings:
-                power = multiply(power, power)
-
-
-def prepare_kernel(mats_ref, raw_ref, parts_ref, *outs):
+        near = powers_of(power, 7)
+        ref[0 : 7 * NP, :] = split_matrix(near)
+        if far:
+            power8 = multiply(block(near, 3), block(near, 3))
+            power16 = multiply(power8, power8)
+            power24 = multiply(power16, power8)
+            ref[7 * NP :, :] = split_matrix(jnp.concatenate([power8, power16, power24], axis=0))
+
+
+def prepare_x_kernel(mats_ref, parts_ref, *outs):
     ux, wx, b0, b1, b2, dx = [mats_ref[NP * k : NP * (k + 1), :] for k in range(6)]
+    parts_ref[...] = split_matrix(powers_of(dx, 6))
+    prepare(CX, False, ux, dx, wx, jnp.concatenate([b0, b1, b2], axis=0), *outs)
+
+
+def prepare_y_kernel(raw_ref, parts_ref, *outs):
     uy, wy, dy = [tiled(raw_ref[k]) for k in range(3)]
-    for k, m in enumerate((dx, uy, wy, dy)):
-        parts_ref[NP * k : NP * (k + 1), :] = split_matrix(m)
-    prepare(CX, 3, ux, dx, wx, jnp.concatenate([b0, b1, b2], axis=0), *outs[:5])
-    prepare(CY, 5, uy, dy, wy, None, *outs[5:])
+    uy2 = multiply(uy, uy)
+    wuy = multiply(jnp.concatenate([wy, uy2], axis=0), uy)
+    wuy2 = multiply(wy, uy2)
+    stacks = [uy, wy, block(wuy, 0), wuy2, block(wuy, 1), powers_of(dy, 4)]
+    parts_ref[...] = split_matrix(jnp.concatenate(stacks, axis=0))
+    prepare(CY, True, uy, dy, wy, None, *outs)
 
 
 def x_rates(coef_ref, which, i):
@@ -189,11 +217,11 @@
     scaled_ref,
     mats_ref,
     raw_y_ref,
-    coef_ref,
     flags_ref,
     coef_y_ref,
     order_ref,
     rhs_ref,
+    coef_ref,
     raw_ref,
     bounds_ref,
     sems,
@@ -218,41 +246,72 @@
         mats_ref[NP * row : NP * (row + 1), :] = value
         return split_matrix(value)
 
-    every = jnp.concatenate(
-        [place(0, raw_ref[0]), place(1, raw_ref[1])] + [place(2 + k, bounds_ref[k]) for k in range(3)],
-        axis=0,
-    )
-    both = every[: 2 * NP]
+    up, scale = place(0, raw_ref[0]), place(1, raw_ref[1])
+    bounds = [place(2 + k, bounds_ref[k]) for k in range(3)]
     down = place(5, raw_ref[2])
+    up_scale = jnp.concatenate([up, scale], axis=0)
+    end_stack = jnp.concatenate([up, scale] + bounds, axis=0)
+    u, w = mats_ref[0:NP, :], mats_ref[NP : 2 * NP, :]
+    d = mats_ref[5 * NP :, :]
+    u2 = multiply(u, u)
+    wu = split_matrix(multiply(w, u))
+    u4 = split_matrix(multiply(u2, u2))
+    u2 = split_matrix(u2)
+    d2 = multiply(d, d)
+    down24 = split_matrix(jnp.concatenate([d2, multiply(d2, d2)], axis=0))
     planes = rhs_ref.reshape(PIECES * NP * 8, LANES)
 
+    ups = [x_rates(coef_ref, 1, i) for i in range(CX)]
+    downs = [x_rates(coef_ref, 0, i) for i in range(CX)]
     flags = row_of(flags_ref[...])
-    carry = 0.0
-    for i in range(CX):
-        k = CY * i // 8
-        if CY * i % 8 == 0:
-            copies[6 + k].wait()
-        start = k * NP * 8 + CY * i % 8
-        f = carry + jnp.concatenate(
+
+    def given(i):
+        start = (CY * i // 8) * NP * 8 + CY * i % 8
+        return jnp.concatenate(
             [planes[pl.ds(start + y, NP, stride=8), :] for y in range(CY)], axis=1
         )
-        if i == 0 or i == CX - 1:
-            out = apply(every, f)
-            ends = out[2 * NP :]
-            chosen = jnp.where(
-                flags == 0, ends[:NP], jnp.where(flags == 1, ends[NP : 2 * NP], ends[2 * NP :])
-            )
-            scaled = jnp.where(rank == (0 if i == 0 else SX - 1), chosen, out[NP : 2 * NP])
-        else:
-            out = apply(both, f)
-            scaled = out[NP:]
-        carry = row_of(x_rates(coef_ref, 1, i)) * out[:NP]
-        scaled_ref[i] = scaled * row_of(1.0 / x_rates(coef_ref, 2, i))
-    f = carry
-    carry = 0.0
-    for i in reversed(range(CX)):
-        carry = row_of(x_rates(coef_ref, 0, i)) * apply(down, scaled_ref[i] + carry)
-    g = carry
+
+    def at_end(i, out):
+        chosen = jnp.where(
+            flags == 0, block(out, 2), jnp.where(flags == 1, block(out, 3), block(out, 4))
+        )
+        return jnp.where(rank == (0 if i == 0 else SX - 1), chosen, block(out, 1))
+
+    def scaled(i, value):
+        value = value * row_of(1.0 / x_rates(coef_ref, 2, i))
+        scaled_ref[i] = value
+        return value
+
+    s, v, part = [None] * CX, [], []
+    for k in range(PIECES):
+        copies[6 + k].wait()
+        out = apply(end_stack if k == 0 else up_scale, given(2 * k))
+        v.append(given(2 * k + 1) + row_of(ups[2 * k]) * block(out, 0))
+        part.append(at_end(0, out) if k == 0 else block(out, 1))
+    two = [None] + [ups[2 * k] * ups[2 * k - 1] for k in range(1, 4)]
+    s[0] = scaled(0, part[0])
+    out = apply(jnp.concatenate([scale, wu, u2], axis=0), v[0])
+    s[1] = scaled(1, block(out, 0))
+    s[2] = scaled(2, part[1] + row_of(ups[1]) * block(out, 1))
+    f3 = v[1] + row_of(two[1]) * block(out, 2)
+    f7 = v[3] + row_of(two[3]) * apply(u2, v[2])
+    out = apply(jnp.concatenate([scale, wu, u2, u4], axis=0), f3)
+    s[3] = scaled(3, block(out, 0))
+    s[4] = scaled(4, part[2] + row_of(ups[3]) * block(out, 1))
+    f5 = v[2] + row_of(two[2]) * block(out, 2)
+    f7 = f7 + row_of(two[3] * two[2]) * block(out, 3)
+    out = apply(jnp.concatenate([scale, wu], axis=0), f5)
+    s[5] = scaled(5, block(out, 0))
+    s[6] = scaled(6, part[3] + row_of(ups[5]) * block(out, 1))
+    out = apply(end_stack, f7)
+    f = row_of(ups[7]) * block(out, 0)
+    s[7] = scaled(7, at_end(7, out))
+    pair = [s[2 * k] + row_of(downs[2 * k + 1]) * apply(down, s[2 * k + 1]) for k in range(4)]
+    two = [downs[2 * k + 1] * downs[2 * k + 2] for k in range(3)]
+    first = pair[0] + row_of(two[0]) * apply(down24[:NP], pair[1])
+    second = pair[2] + row_of(two[2]) * apply(down24[:NP], pair[3])
+    g = first + row_of(two[0] * two[1]) * apply(down24[NP:], second)
+    g = row_of(downs[0]) * apply(down, g)
     for copy in copies[6 + PIECES :]:
         copy.wait()
     for y, (fy, gy) in enumerate(zip(columns(f), columns(g))):
@@ -302,6 +361,7 @@
         shifted(f, 1, width, ncol, False),
         shifted(up_rate, 1, width, ncol, False),
         up_ref,
+        (7,),
         width,
         ncol,
         False,
@@ -321,6 +381,7 @@
         shifted(g, 1, width, ncol, True),
         shifted(down_rate, 1, width, ncol, True),
         down_ref,
+        (7,),
         width,
         ncol,
         True,
@@ -343,6 +404,7 @@
     coef_ref,
     flags_ref,
     parts_ref,
+    parts_y_ref,
     from_ref,
     in_ref,
     coef_y_ref,
@@ -353,7 +415,11 @@
 ):
     rank = rank_ref[0]
     parts = parts_ref[...]
-    down, both_y, down_y = parts[:NP], parts[NP : 3 * NP], parts[3 * NP :]
+    parts_y = parts_y_ref[...]
+    down = parts
+    u_y, w_y, wu_y, wu2_y, u3_y = [block(parts_y, k) for k in range(5)]
+    up_scale_y = parts_y[: 2 * NP]
+    down_y = parts_y[5 * NP :]
     hs, es = [], []
     for y in range(CY):
         h, e = regroup([in_ref[2 * y], in_ref[2 * y + 1]], NP)
@@ -364,8 +430,9 @@
     up_rates = [jnp.ones((CY, LANES), F32)]
     for i in range(CX - 1):
         up_rates.append(up_rates[-1] * x_rates(coef_ref, 1, i))
-    carry = jnp.concatenate(es, axis=1)
-    for i in reversed(range(CX)):
+    downs = [x_rates(coef_ref, 0, i) for i in range(CX)]
+
+    def scaled(i):
         term = through[NP * i : NP * (i + 1)]
         if i == CX - 1:
             ends = through[NP * CX :]
@@ -373,11 +440,30 @@
                 flags == 0, ends[:NP], jnp.where(flags == 1, ends[NP : 2 * NP], ends[2 * NP :])
             )
             term = jnp.where(rank == SX - 1, chosen, term)
-        g = local_ref[i] + row_of(up_rates[i] / x_rates(coef_ref, 2, i)) * term + carry
+        return local_ref[i] + row_of(up_rates[i] / x_rates(coef_ref, 2, i)) * term
+
+    def keep(i, g):
         for y in range(CY):
             adj_ref[y, :, LANES * i : LANES * (i + 1)] = g[:, LANES * y : LANES * (y + 1)]
-        if i > 0:
-            carry = row_of(x_rates(coef_ref, 0, i)) * apply(down, g)
+
+    s = [scaled(i) for i in range(CX)]
+    s[7] = s[7] + jnp.concatenate(es, axis=1)
+    keep(7, s[7])
+    pair = [s[2 * k] + row_of(downs[2 * k + 1]) * apply(block(down, 0), s[2 * k + 1]) for k in range(4)]
+    two = [downs[2 * k + 1] * downs[2 * k + 2] for k in range(3)]
+    g = [pair[0], s[1], pair[1], s[3], pair[2], s[5]]
+    for k in (3, 2, 1):
+        out = apply(down[: 2 * k * NP], pair[k])
+        weight = None
+        for j in reversed(range(k)):
+            odd = downs[2 * j + 2] if weight is None else weight * downs[2 * j + 2]
+            weight = two[j] if weight is None else weight * two[j]
+            power = 2 * (k - j)
+            g[2 * j + 1] = g[2 * j + 1] + row_of(odd) * block(out, power - 2)
+            g[2 * j] = g[2 * j] + row_of(weight) * block(out, power - 1)
+    for i in range(6):
+        keep(i, g[i])
+    keep(6, pair[3])
 
     flip = order_ref[...] > 0
     flip_row = row_of(order_ref[...]) > 0
@@ -385,16 +471,29 @@
     def oriented(which, p):
         return y_rates(coef_y_ref, which, flip, p)
 
-    carry = 0.0
+    a = [jnp.where(flip_row, adj_ref[CY - 1 - p], adj_ref[p]) for p in range(CY)]
+    ups = [oriented(1, p) for p in range(CY)]
+    downs = [oriented(0, p) for p in range(CY)]
+    inverse = [row_of(1.0 / oriented(2, p)) for p in range(CY)]
+    out = apply(up_scale_y, a[0])
+    f1 = a[1] + row_of(ups[0]) * block(out, 0)
+    s = [block(out, 1)]
+    out2 = apply(up_scale_y, a[2])
+    v3 = a[3] + row_of(ups[2]) * block(out2, 0)
+    out1 = apply(jnp.concatenate([w_y, wu_y, wu2_y, u3_y], axis=0), f1)
+    out3 = apply(up_scale_y, v3)
+    two = ups[1] * ups[2]
+    s.append(block(out1, 0))
+    s.append(block(out2, 1) + row_of(ups[1]) * block(out1, 1))
+    s.append(block(out3, 1) + row_of(two) * block(out1, 2))
+    f = row_of(ups[3]) * block(out3, 0) + row_of(ups[3] * two) * block(out1, 3)
+    g, weight = 0.0, downs[0]
     for p in range(CY):
-        out = apply(both_y, jnp.where(flip_row, adj_ref[CY - 1 - p], adj_ref[p]) + carry)
-        carry = row_of(oriented(1, p)) * out[:NP]
-        scaled_ref[p] = out[NP:] * row_of(1.0 / oriented(2, p))
-    f = carry
-    carry = 0.0
-    for p in reversed(range(CY)):
-        carry = row_of(oriented(0, p)) * apply(down_y, scaled_ref[p] + carry)
-    g = carry
+        value = s[p] * inverse[p]
+        scaled_ref[p] = value
+        g = g + row_of(weight) * apply(block(down_y, p), value)
+        if p + 1 < CY:
+            weight = weight * downs[p + 1]
 
     down_rate = oriented(0, 0)
     up_rate = jnp.ones_like(down_rate)
@@ -438,6 +537,7 @@
         shifted(f, 1, width, ncol, False),
         shifted(up_rate, 1, width, ncol, False),
         up_ref,
+        (7, 3),
         width,
         ncol,
         False,
@@ -449,6 +549,7 @@
         shifted(g, 1, width, ncol, True),
         shifted(down_rate, 1, width, ncol, True),
         down_ref,
+        (7, 3),
         width,
         ncol,
         True,
@@ -462,7 +563,7 @@
 
 
 def y_final_kernel(local_ref, coef_y_ref, order_ref, parts_ref, from_ref, in_ref, out_ref, solved_ref):
-    down = parts_ref[3 * NP :, :]
+    down = parts_ref[5 * NP : 8 * NP, :]
     flip = order_ref[...] > 0
     flip_row = row_of(order_ref[...]) > 0
 
@@ -478,17 +579,25 @@
     up_rates = [jnp.ones((CX, LANES), F32)]
     for p in range(CY - 1):
         up_rates.append(up_rates[-1] * oriented(1, p))
-    carry = jnp.concatenate(es, axis=1)
-    for p in reversed(range(CY)):
+    downs = [oriented(0, p) for p in range(CY)]
+    s = []
+    for p in range(CY):
         term = row_of(up_rates[p] / oriented(2, p)) * through[NP * p : NP * (p + 1)]
-        g = local_ref[p] + term + carry
-        solved_ref[p] = g
-        if p > 0:
-            carry = row_of(oriented(0, p)) * apply(down, g)
+        s.append(local_ref[p] + term)
+    s[3] = s[3] + jnp.concatenate(es, axis=1)
+    g = list(s)
+    for p in (3, 2, 1):
+        out = apply(down[: NP * p], s[p])
+        weight = None
+        for j in reversed(range(p)):
+            weight = downs[j + 1] if weight is None else weight * downs[j + 1]
+            g[j] = g[j] + row_of(weight) * block(out, p - 1 - j)
+    for p in range(CY):
+        solved_ref[p] = g[p]
     for y in range(CY):
         plane = jnp.where(flip_row, solved_ref[CY - 1 - y], solved_ref[y])
-        for x, block in enumerate(columns(plane)):
-            out_ref[pl.ds(CY * x + y, NP, stride=CX * CY), :] = block
+        for x, piece in enumerate(columns(plane)):
+            out_ref[pl.ds(CY * x + y, NP, stride=CX * CY), :] = piece
 
 
 def in_hbm(a):
@@ -514,12 +623,12 @@
     )
 
 
-def prepared_shapes(cells, extra, doublings):
+def prepared_shapes(cells, extra, powers):
     return (
         shape((cells + extra) * NP, 4 * NP, dtype=BF16),
         shape((cells + extra) * NP, 4 * NP, dtype=BF16),
-        shape(doublings, NP, 4 * NP, dtype=BF16),
-        shape(doublings, NP, 4 * NP, dtype=BF16),
+        shape(powers * NP, 4 * NP, dtype=BF16),
+        shape(powers * NP, 4 * NP, dtype=BF16),
         shape(8, LANES),
     )
 
@@ -552,14 +661,13 @@
     coef_x = coef_x.reshape(3, CX * CY, LANES)
     coef_y = coef_y.reshape(3, CX * CY, LANES)
 
-    sent, local, tiles, raw_y, coef_x, flags, coef_y, order = call(
+    sent, local, tiles, raw_y, flags, coef_y, order = call(
         x_local_kernel,
         (
             shape(SX, NP + 8, LANES),
             shape(CX, NP, CY * LANES),
             shape(6 * NP, 4 * NP),
             shape(3, NP, NP),
-            shape(3, CX * CY, LANES),
             shape(CY, LANES, dtype=jnp.int32),
             shape(3, CX * CY, LANES),
             shape(CX, LANES, dtype=jnp.int32),
@@ -567,6 +675,7 @@
         12,
         [
             pltpu.VMEM((PIECES, NP, 8, LANES), F32),
+            pltpu.VMEM((3, CX * CY, LANES), F32),
             pltpu.VMEM((3, NP, NP), F32),
             pltpu.VMEM((3, NP, NP), F32),
             pltpu.SemaphoreType.DMA((11 + PIECES,)),
@@ -575,19 +684,26 @@
         pltpu.HBM,
     )(rank, *[in_hbm(a) for a in (rhs, coef_x, bc_flags) + mats + (coef_y, line_order)])
     got = lax.all_to_all(sent, "gx", 0, 0, tiled=True)
-    prep_shapes = (shape(4 * NP, 4 * NP, dtype=BF16),)
-    prep_shapes += prepared_shapes(CX, 3, 3) + prepared_shapes(CY, 0, 5)
-    prep = call(prepare_kernel, prep_shapes, 2)(tiles, raw_y)
-    parts, gain_x, from_x, up_x, down_x, norm_x, gain_y, from_y, up_y, down_y, norm_y = prep
+    parts_x, gain_x, from_x, up_x, down_x, norm_x = call(
+        prepare_x_kernel,
+        (shape(6 * NP, 4 * NP, dtype=BF16),) + prepared_shapes(CX, 3, 7),
+        1,
+    )(tiles)
     back = call(x_owner_kernel, shape(SX, NP, LANES), 5)(got, gain_x, up_x, down_x, norm_x)
+    raw_y, back = lax.optimization_barrier((raw_y, back))
     terms = lax.all_to_all(back, "gx", 0, 0, tiled=True)
+    parts_y, gain_y, from_y, up_y, down_y, norm_y = call(
+        prepare_y_kernel,
+        (shape(9 * NP, 4 * NP, dtype=BF16),) + prepared_shapes(CY, 0, 10),
+        1,
+    )(raw_y)
     local, sent = call(
         middle_kernel,
         (shape(CY, NP, CX * LANES), shape(SY * ROWS, LANES)),
-        8,
+        9,
         [pltpu.VMEM((CY, NP, CX * LANES), F32)],
         1,
-    )(rank, local, coef_x, flags, parts, from_x, terms, coef_y, order)
+    )(rank, local, coef_x, flags, parts_x, parts_y, from_x, terms, coef_y, order)
     got = lax.all_to_all(sent.reshape(SY, ROWS // 2, 2, LANES), "gy", 0, 0, tiled=True)
     back = call(
         y_owner_kernel, shape(SY, 32, LANES), 5, [pltpu.VMEM((SY, 32, LANES), F32)]
@@ -598,7 +714,7 @@
         shape(NP * CX * CY, LANES),
         6,
         [pltpu.VMEM((CY, NP, CX * LANES), F32)],
-    )(local, coef_y, order, parts, from_y, terms)
+    )(local, coef_y, order, parts_y, from_y, terms)
     return out.reshape(NP, CX, CY, LANES)
 
 

time: 89.5 us -> 88.1 us (0.984)
  blocking collectives: 60.7 us -> 50.6 us
  waiting for transfers between devices: 4.06 us -> 9.8 us
  starting transfers between devices: 4.3 us -> 7.73 us
    all_to_all x1 -> x0, blocking collectives: 10.1 us -> none  [per_device(): terms = lax.all_to_all(back, 'gx', 0, 0, tiled=True)]
    all_to_all x0 -> x1, waiting for transfers between devices: none -> 5.01 us  [per_device(): terms = lax.all_to_all(back, 'gx', 0, 0, tiled=True)]
    all_to_all x0 -> x1, starting transfers between devices: none -> 3.41 us  [per_device(): terms = lax.all_to_all(back, 'gx', 0, 0, tiled=True)]
    pallas_call x1 -> x2, Pallas kernels: 3.83 us -> 5.53 us  [the longest x1 3.1 us: per_device(): call(prepare_x_kernel, (shape(6 * NP, 4 * NP, dtype=BF16),) + prepared_sh...]
    pallas_call x1, Pallas kernels: 3.18 us -> 2.11 us  [per_device(): call(middle_kernel, (shape(CY, NP, CX * LANES), shape(SY * ROWS, LANES)),...]
  transfers between devices with their start and end apart: 1 -> 2, of which waited for: 1 -> 2; matrix products, arithmetic and copies ran while one was open for 0% -> 0% of each run, Pallas kernels for 4% -> 6%
where the time goes in v2:
time: 88.1 us; the launch traced here: 87.7 us
  blocking collectives  50.6 us (57%)
  Pallas kernels  19.5 us (22%)
  waiting for transfers between devices  9.8 us (11%)
  starting transfers between devices  7.73 us (9%)
    all_to_all x1, blocking collectives, per_device(): lax.all_to_all(sent.reshape(SY, ROWS // 2, 2, LANES), 'gy', 0, 0, tiled=T...  29.1 us
    all_to_all x1, blocking collectives, per_device(): terms = lax.all_to_all(back, 'gy', 0, 0, tiled=True)  21.6 us
    all_to_all x1, waiting for transfers between devices, per_device(): terms = lax.all_to_all(back, 'gx', 0, 0, tiled=True)  5.01 us
    all_to_all x1, waiting for transfers between devices, per_device(): got = lax.all_to_all(sent, 'gx', 0, 0, tiled=True)  4.79 us
    pallas_call x1, Pallas kernels, per_device(): call(x_local_kernel, (shape(SX, NP + 8, LANES), shape(CX, NP, CY * LANES)...  4.66 us
    all_to_all x1, starting transfers between devices, per_device(): got = lax.all_to_all(sent, 'gx', 0, 0, tiled=True)  4.32 us
    all_to_all x1, starting transfers between devices, per_device(): terms = lax.all_to_all(back, 'gx', 0, 0, tiled=True)  3.41 us
    pallas_call x1, Pallas kernels, per_device(): call(prepare_x_kernel, (shape(6 * NP, 4 * NP, dtype=BF16),) + prepared_sh...  3.1 us
  transfers between devices with their start and end apart: 2, of which 2 were waited for; matrix products, arithmetic and copies ran while one was open for 0% of the time, Pallas kernels for 6%

profile of v2, /device:TPU:32, one launch (start us, length us, event | category | flops | bytes accessed | tf_op | source)
XLA Modules:
  0.0 87.7 jit_solution(7238033716043577494)
XLA Ops:
  0.0 4.7 %shard_map.118 = (f32[8,72,128]{2,1,0:T(8,128)}, f32[8,64,512]{2,1,0:T(8,128)S(1)}, f32[384,256]{1,0:T(8,128)S(1)}, f32[3,64,64]{2,1,0:T(8,128)S(1)}, s32[4,128]...) custom-call(s32[1]{0:T(128)} %bitcast.rank_ref, f32[64,32,128]{2,1,0:T(8,128)} %bitcast.11, ...), custom_call_target="tpu_custom_call" | custom-call | tf_op jit(solution)/shard_map/pallas_call | solution.py:664
  4.7 4.3 %all-to-all-start = ((f32[8,72,128]{2,1,0:T(8,128)}), f32[8,72,128]{2,1,0:T(8,128)S(1)}, u32[]{:S(2)}, u32[]{:S(2)}) async-start(f32[8,72,128]{2,1,0:T(8,128)} %get-tuple-element.33), calls=%async_computation | async-start | bytes 589824 | tf_op jit(solution)/shard_map/all_to_all | solution.py:686
  9.0 3.1 %shard_map.119 = (bf16[384,256]{1,0:T(8,128)(2,1)S(1)}, bf16[704,256]{1,0:T(8,128)(2,1)S(1)}, bf16[704,256]{1,0:T(8,128)(2,1)S(1)}, bf16[448,256]{1,0:T(8,128)(2...) custom-call(f32[384,256]{1,0:T(8,128)S(1)} %get-tuple-element.30.mats_ref), custom_call_target="tpu_custom_call" | custom-call | tf_op jit(solution)/shard_map/pallas_call | solution.py:687
  12.1 4.8 %all-to-all-done.in_ref = f32[8,72,128]{2,1,0:T(8,128)S(1)} async-done(((f32[8,72,128]{2,1,0:T(8,128)}), f32[8,72,128]{2,1,0:T(8,128)S(1)}, u32[]{:S(2)}, u32[]{:S(2)}) %all-to-all-start) | async-done | bytes 294944 | tf_op jit(solution)/shard_map/all_to_all | solution.py:686
  16.9 2.0 %shard_map.120 = f32[8,64,128]{2,1,0:T(8,128)} custom-call(f32[8,72,128]{2,1,0:T(8,128)S(1)} %all-to-all-done.in_ref, bf16[704,256]{1,0:T(8,128)(2,1)S(1)} %get-tuple-element.34.gain_ref, bf16[448,256]{1,0:T(8,128)(2,1)S(1)} %get-tuple-element.35.up_ref, bf16[448,256]{1,0:T(8,128)(2,1)S(1)} %get-tuple-element.36.down_ref, ...), custom_call_target="tpu_custom_call" | custom-call | tf_op jit(solution)/shard_map/pallas_call | solution.py:692
  18.8 3.4 %all-to-all-start.1 = ((f32[8,64,128]{2,1,0:T(8,128)}), f32[8,64,128]{2,1,0:T(8,128)S(1)}, u32[]{:S(2)}, u32[]{:S(2)}) async-start(f32[8,64,128]{2,1,0:T(8,128)} %shard_map.120), calls=%async_computation.1 | async-start | bytes 524288 | tf_op jit(solution)/shard_map/all_to_all | solution.py:694
  22.3 0.0 copy-start
  22.3 2.4 %shard_map.121 = (bf16[576,256]{1,0:T(8,128)(2,1)S(1)}, bf16[256,256]{1,0:T(8,128)(2,1)S(1)}, bf16[256,256]{1,0:T(8,128)(2,1)S(1)}, bf16[640,256]{1,0:T(8,128)(2...) custom-call(f32[3,64,64]{2,1,0:T(8,128)S(1)} %get-tuple-element.38.raw_ref), custom_call_target="tpu_custom_call" | custom-call | tf_op jit(solution)/shard_map/pallas_call | solution.py:695
  24.7 5.0 %all-to-all-done.1.in_ref = f32[8,64,128]{2,1,0:T(8,128)S(1)} async-done(((f32[8,64,128]{2,1,0:T(8,128)}), f32[8,64,128]{2,1,0:T(8,128)S(1)}, u32[]{:S(2)}, u32[]{:S(2)}) %all-to-all-start.1) | async-done | bytes 262176 | tf_op jit(solution)/shard_map/all_to_all | solution.py:694
  29.7 0.0 copy-done
  29.7 2.1 %shard_map.122 = (f32[4,64,1024]{2,1,0:T(8,128)S(1)}, f32[1088,128]{1,0:T(8,128)S(1)}) custom-call(s32[1]{0:T(128)} %bitcast.rank_ref, f32[8,64,512]{2,1,0:T(8,128)S(1)} %get-tuple-element.28.local_ref, f32[3,32,128]{2,1,0:T(8,128)S(1)} %bitcast.10, s32[4,128]{1,0:T(4,128)S(1)} %get-tuple-element.29.flags_ref, ...), custom_call_target="tpu_custom_call" | custom-call | tf_op jit(solution)/shard_map/pallas_call | solution.py:700
  31.8 29.1 %all_to_all.20 = f32[32,17,2,128]{3,2,1,0:T(2,128)S(1)} all-to-all(f32[32,17,2,128]{3,2,1,0:T(2,128)S(1)} %bitcast.8), channel_id=1, replica_groups=mesh['gx'=8,'gy'=32] {'gy'}, dimensions={0} | all-to-all | bytes 1114112 | tf_op jit(solution)/shard_map/all_to_all | solution.py:707
  60.9 2.8 %shard_map.123 = f32[32,32,128]{2,1,0:T(8,128)S(1)} custom-call(f32[1088,128]{1,0:T(8,128)S(1)} %bitcast.7, bf16[256,256]{1,0:T(8,128)(2,1)S(1)} %get-tuple-element.47.gain_ref, bf16[640,256]{1,0:T(8,128)(2,1)S(1)} %get-tuple-element.48.up_ref, bf16[640,256]{1,0:T(8,128)(2,1)S(1)} %get-tuple-element.49.down_ref, f32[8,128]{1,0:T(8,128)S(1)} %get-tuple-element.50.norm_ref), custom_call_target="tpu_custom_call" | custom-call | tf_op jit(solution)/shard_map/pallas_call | solution.py:708
  63.7 21.6 %all_to_all.21.in_ref = f32[32,32,128]{2,1,0:T(8,128)S(1)} all-to-all(f32[32,32,128]{2,1,0:T(8,128)S(1)} %shard_map.123), channel_id=1, replica_groups=mesh['gx'=8,'gy'=32] {'gy'}, dimensions={0} | all-to-all | bytes 1048576 | tf_op jit(solution)/shard_map/all_to_all | solution.py:711
  85.3 2.5 %shard_map.124 = f32[2048,128]{1,0:T(8,128)} custom-call(f32[4,64,1024]{2,1,0:T(8,128)S(1)} %get-tuple-element.44.local_ref, f32[3,32,128]{2,1,0:T(8,128)S(1)} %get-tuple-element.42.coef_y_ref, s32[8,128]{1,0:T(8,128)S(1)} %get-tuple-element.43.order_ref, bf16[576,256]{1,0:T(8,128)(2,1)S(1)} %get-tuple-element.39.parts_y_ref.parts_ref, ...), custom_call_target="tpu_custom_call" | custom-call | tf_op jit(solution)/shard_map/pallas_call | solution.py:712
Async XLA Ops:
  4.7 12.2 %all-to-all-start = ((f32[8,72,128]{2,1,0:T(8,128)}), f32[8,72,128]{2,1,0:T(8,128)S(1)}, u32[]{:S(2)}, u32[]{:S(2)}) async-start(f32[8,72,128]{2,1,0:T(8,128)} %get-tuple-element.33), calls=%async_computation | async-start | bytes 589824 | tf_op jit(solution)/shard_map/all_to_all | solution.py:686
  18.8 10.9 %all-to-all-start.1 = ((f32[8,64,128]{2,1,0:T(8,128)}), f32[8,64,128]{2,1,0:T(8,128)S(1)}, u32[]{:S(2)}, u32[]{:S(2)}) async-start(f32[8,64,128]{2,1,0:T(8,128)} %shard_map.120), calls=%async_computation.1 | async-start | bytes 524288 | tf_op jit(solution)/shard_map/all_to_all | solution.py:694
  22.3 7.5 %copy-start = (f32[3,8,4,128]{3,2,1,0:T(4,128)S(1)}, f32[3,8,4,128]{3,2,1,0:T(4,128)}, u32[]{:S(2)}) copy-start(f32[3,8,4,128]{3,2,1,0:T(4,128)} %param.13) | copy-start | bytes 147460

commit v3 on v2

--- a/solution.py
+++ b/solution.py
@@ -9,6 +9,7 @@
 LANES = 128
 CX = 8
 PIECES = 4
+HALVES = 2
 CY = 4
 SX = 8
 SY = 32
@@ -143,56 +144,51 @@
 
 def prepare(cells, far, up, down, scale, bounds, gain_ref, from_ref, up_ref, down_ref, norm_ref):
     halves = cells.bit_length() - 1
-    ups, downs = [up], [down]
+    ups = [up]
     for _ in range(halves):
         ups.append(multiply(ups[-1], ups[-1]))
-        downs.append(multiply(downs[-1], downs[-1]))
     scaled = scale
-    stack = down
     for k in range(halves):
         scaled = jnp.concatenate([scaled, multiply(scaled, ups[k])], axis=0)
-        stack = jnp.concatenate([stack, multiply(stack, downs[k])], axis=0)
+    downs = powers_of(down, cells)
+    stack = split_matrix(downs)
     from_ref[0 : cells * NP, :] = split_matrix(scaled)
     for j in range(cells):
-        rows = slice(NP * j, NP * (j + 1))
-        gain_ref[rows, :] = split_matrix(multiply(stack[rows], scaled[rows]))
+        gain = apply(block(stack, j), block(scaled, j))
+        gain_ref[NP * j : NP * (j + 1), :] = split_matrix(gain)
     if bounds is not None:
         for k in range(halves):
             bounds = multiply(bounds, ups[k])
         from_ref[cells * NP :, :] = split_matrix(bounds)
         for kind in range(3):
-            rows = slice(NP * (cells + kind), NP * (cells + kind + 1))
-            ends = bounds[NP * kind : NP * (kind + 1)]
-            gain_ref[rows, :] = split_matrix(multiply(downs[halves], ends))
+            gain = apply(block(stack, cells - 1), block(bounds, kind))
+            gain_ref[NP * (cells + kind) : NP * (cells + kind + 1), :] = split_matrix(gain)
     norm_ref[...] = jnp.zeros(norm_ref.shape, F32)
-    for row, (power, ref) in enumerate(((ups[halves], up_ref), (downs[halves], down_ref))):
+    tops = ((ups[halves], up_ref), (block(downs, cells - 1), down_ref))
+    for row, (power, ref) in enumerate(tops):
         norm = jnp.max(jnp.sum(jnp.abs(power[:, :NP]), axis=1, keepdims=True), axis=0, keepdims=True)
         norm = jnp.maximum(norm, 1e-30)
         norm_ref[row : row + 1, :] = jnp.broadcast_to(norm, (1, LANES))
-        power = power / norm
-        near = powers_of(power, 7)
+        near = powers_of(power / norm, 7)
         ref[0 : 7 * NP, :] = split_matrix(near)
         if far:
             power8 = multiply(block(near, 3), block(near, 3))
             power16 = multiply(power8, power8)
             power24 = multiply(power16, power8)
             ref[7 * NP :, :] = split_matrix(jnp.concatenate([power8, power16, power24], axis=0))
-
-
-def prepare_x_kernel(mats_ref, parts_ref, *outs):
+    return ups, scaled, stack
+
+
+def prepare_kernel(mats_ref, raw_ref, parts_ref, parts_y_ref, *outs):
     ux, wx, b0, b1, b2, dx = [mats_ref[NP * k : NP * (k + 1), :] for k in range(6)]
-    parts_ref[...] = split_matrix(powers_of(dx, 6))
-    prepare(CX, False, ux, dx, wx, jnp.concatenate([b0, b1, b2], axis=0), *outs)
-
-
-def prepare_y_kernel(raw_ref, parts_ref, *outs):
+    bounds = jnp.concatenate([b0, b1, b2], axis=0)
+    _, _, stack = prepare(CX, False, ux, dx, wx, bounds, *outs[:5])
+    parts_ref[...] = stack[: 6 * NP]
     uy, wy, dy = [tiled(raw_ref[k]) for k in range(3)]
-    uy2 = multiply(uy, uy)
-    wuy = multiply(jnp.concatenate([wy, uy2], axis=0), uy)
-    wuy2 = multiply(wy, uy2)
-    stacks = [uy, wy, block(wuy, 0), wuy2, block(wuy, 1), powers_of(dy, 4)]
-    parts_ref[...] = split_matrix(jnp.concatenate(stacks, axis=0))
-    prepare(CY, True, uy, dy, wy, None, *outs)
+    ups, scaled, stack = prepare(CY, True, uy, dy, wy, None, *outs[5:])
+    extra = [uy, scaled[: 3 * NP], multiply(ups[1], uy)]
+    parts_y_ref[0 : 5 * NP, :] = split_matrix(jnp.concatenate(extra, axis=0))
+    parts_y_ref[5 * NP :, :] = stack
 
 
 def x_rates(coef_ref, which, i):
@@ -562,42 +558,55 @@
         out_ref[s] = jnp.where(flip, res_ref[SY - 1 - s], res_ref[s])
 
 
-def y_final_kernel(local_ref, coef_y_ref, order_ref, parts_ref, from_ref, in_ref, out_ref, solved_ref):
+def y_final_kernel(
+    local_ref, coef_y_ref, order_ref, parts_ref, from_ref, in_ref, out_hbm, out_ref, sems
+):
     down = parts_ref[5 * NP : 8 * NP, :]
     flip = order_ref[...] > 0
-    flip_row = row_of(order_ref[...]) > 0
 
     def oriented(which, p):
         return y_rates(coef_y_ref, which, flip, p)
 
-    hs, es = [], []
-    for x in range(CX):
-        outs = regroup([in_ref[4 * x + a] for a in range(4)], 32)
-        hs.append(jnp.concatenate(outs[:2], axis=0))
-        es.append(jnp.concatenate(outs[2:], axis=0))
-    through = apply(from_ref[...], jnp.concatenate(hs, axis=1))
     up_rates = [jnp.ones((CX, LANES), F32)]
     for p in range(CY - 1):
         up_rates.append(up_rates[-1] * oriented(1, p))
+    term_rates = [up_rates[p] / oriented(2, p) for p in range(CY)]
     downs = [oriented(0, p) for p in range(CY)]
-    s = []
-    for p in range(CY):
-        term = row_of(up_rates[p] / oriented(2, p)) * through[NP * p : NP * (p + 1)]
-        s.append(local_ref[p] + term)
-    s[3] = s[3] + jnp.concatenate(es, axis=1)
-    g = list(s)
-    for p in (3, 2, 1):
-        out = apply(down[: NP * p], s[p])
-        weight = None
-        for j in reversed(range(p)):
-            weight = downs[j + 1] if weight is None else weight * downs[j + 1]
-            g[j] = g[j] + row_of(weight) * block(out, p - 1 - j)
-    for p in range(CY):
-        solved_ref[p] = g[p]
-    for y in range(CY):
-        plane = jnp.where(flip_row, solved_ref[CY - 1 - y], solved_ref[y])
-        for x, piece in enumerate(columns(plane)):
-            out_ref[pl.ds(CY * x + y, NP, stride=CX * CY), :] = piece
+    part = CX // HALVES
+    copies = []
+    for half in range(HALVES):
+        first = part * half
+        lanes = slice(LANES * first, LANES * (first + part))
+
+        def row(rate):
+            return row_of(rate[first : first + part])
+
+        hs, es = [], []
+        for x in range(first, first + part):
+            outs = regroup([in_ref[4 * x + a] for a in range(4)], 32)
+            hs.append(jnp.concatenate(outs[:2], axis=0))
+            es.append(jnp.concatenate(outs[2:], axis=0))
+        through = apply(from_ref[...], jnp.concatenate(hs, axis=1))
+        s = [local_ref[p, :, lanes] + row(term_rates[p]) * block(through, p) for p in range(CY)]
+        s[3] = s[3] + jnp.concatenate(es, axis=1)
+        g = list(s)
+        for p in (3, 2, 1):
+            out = apply(down[: NP * p], s[p])
+            weight = None
+            for j in reversed(range(p)):
+                weight = downs[j + 1] if weight is None else weight * downs[j + 1]
+                g[j] = g[j] + row(weight) * block(out, p - 1 - j)
+        flip_row = row_of(order_ref[first : first + part, :]) > 0
+        planes = out_ref.at[half].reshape(NP * CY * part, LANES)
+        for y in range(CY):
+            plane = jnp.where(flip_row, g[CY - 1 - y], g[y])
+            for x, piece in enumerate(columns(plane)):
+                planes[pl.ds(CY * x + y, NP, stride=CY * part), :] = piece
+        target = out_hbm.at[:, CY * first : CY * (first + part), :]
+        copies.append(pltpu.make_async_copy(out_ref.at[half], target, sems.at[half]))
+        copies[-1].start()
+    for copy in copies:
+        copy.wait()
 
 
 def in_hbm(a):
@@ -608,8 +617,8 @@
     return jax.ShapeDtypeStruct(dims, dtype)
 
 
-def call(kernel, out_shape, n_in, scratch=(), scalars=0, space=pltpu.VMEM):
-    whole = pl.BlockSpec(memory_space=pltpu.VMEM)
+def call(kernel, out_shape, n_in, scratch=(), scalars=0, space=pltpu.VMEM, out_space=pltpu.VMEM):
+    whole = pl.BlockSpec(memory_space=out_space)
     specs = [pl.BlockSpec(memory_space=pltpu.SMEM)] * scalars
     specs += [pl.BlockSpec(memory_space=space)] * n_in
     outs = jax.tree.map(lambda _: whole, out_shape)
@@ -684,19 +693,15 @@
         pltpu.HBM,
     )(rank, *[in_hbm(a) for a in (rhs, coef_x, bc_flags) + mats + (coef_y, line_order)])
     got = lax.all_to_all(sent, "gx", 0, 0, tiled=True)
-    parts_x, gain_x, from_x, up_x, down_x, norm_x = call(
-        prepare_x_kernel,
-        (shape(6 * NP, 4 * NP, dtype=BF16),) + prepared_shapes(CX, 3, 7),
-        1,
-    )(tiles)
+    prep_shapes = (shape(6 * NP, 4 * NP, dtype=BF16), shape(9 * NP, 4 * NP, dtype=BF16))
+    prep = call(
+        prepare_kernel, prep_shapes + prepared_shapes(CX, 3, 7) + prepared_shapes(CY, 0, 10), 2
+    )(tiles, raw_y)
+    parts_x, parts_y = prep[:2]
+    gain_x, from_x, up_x, down_x, norm_x = prep[2:7]
+    gain_y, from_y, up_y, down_y, norm_y = prep[7:]
     back = call(x_owner_kernel, shape(SX, NP, LANES), 5)(got, gain_x, up_x, down_x, norm_x)
-    raw_y, back = lax.optimization_barrier((raw_y, back))
     terms = lax.all_to_all(back, "gx", 0, 0, tiled=True)
-    parts_y, gain_y, from_y, up_y, down_y, norm_y = call(
-        prepare_y_kernel,
-        (shape(9 * NP, 4 * NP, dtype=BF16),) + prepared_shapes(CY, 0, 10),
-        1,
-    )(raw_y)
     local, sent = call(
         middle_kernel,
         (shape(CY, NP, CX * LANES), shape(SY * ROWS, LANES)),
@@ -711,9 +716,13 @@
     terms = lax.all_to_all(back, "gy", 0, 0, tiled=True)
     out = call(
         y_final_kernel,
-        shape(NP * CX * CY, LANES),
+        shape(NP, CX * CY, LANES),
         6,
-        [pltpu.VMEM((CY, NP, CX * LANES), F32)],
+        [
+            pltpu.VMEM((HALVES, NP, CX * CY // HALVES, LANES), F32),
+            pltpu.SemaphoreType.DMA((HALVES,)),
+        ],
+        out_space=pltpu.HBM,
     )(local, coef_y, order, parts_y, from_y, terms)
     return out.reshape(NP, CX, CY, LANES)
 

time: 88.1 us -> 94.5 us (1.073)
  blocking collectives: 50.6 us -> 63.2 us
  waiting for transfers between devices: 9.8 us -> 0.01 us
  local copies, waits for them, and re-layouts: 0.01 us -> 9.01 us
  starting transfers between devices: 7.73 us -> 4.3 us
  Pallas kernels: 19.5 us -> 17.4 us
    all_to_all x0 -> x1, blocking collectives: none -> 12.3 us  [per_device(): terms = lax.all_to_all(back, 'gx', 0, 0, tiled=True)]
    unnamed x2 -> x38, local copies, waits for them, and re-layouts: 0.01 us -> 9.01 us
    all_to_all x1 -> x0, waiting for transfers between devices: 5.01 us -> none  [per_device(): terms = lax.all_to_all(back, 'gx', 0, 0, tiled=True)]
    all_to_all x1, waiting for transfers between devices: 4.79 us -> 0.01 us  [per_device(): got = lax.all_to_all(sent, 'gx', 0, 0, tiled=True)]
    all_to_all x1 -> x0, starting transfers between devices: 3.41 us -> none  [per_device(): terms = lax.all_to_all(back, 'gx', 0, 0, tiled=True)]
    pallas_call x3 -> x2, Pallas kernels: 7.99 us -> 6.63 us  [the longest x1 4.56 us: per_device(): call(prepare_kernel, prep_shapes + prepared_shapes(CX, 3, 7) + prepared_s...]
  transfers between devices with their start and end apart: 2 -> 1, of which waited for: 2 -> 0; matrix products, arithmetic and copies ran while one was open for 0% -> 0% of each run, Pallas kernels for 6% -> 5%
where the time goes in v3:
time: 94.5 us; the launch traced here: 94 us
  blocking collectives  63.2 us (67%)
  Pallas kernels  17.4 us (18%)
  local copies, waits for them, and re-layouts  9.01 us (10%)
  starting transfers between devices  4.3 us (5%)
    all_to_all x1, blocking collectives, per_device(): lax.all_to_all(sent.reshape(SY, ROWS // 2, 2, LANES), 'gy', 0, 0, tiled=T...  29.2 us
    all_to_all x1, blocking collectives, per_device(): terms = lax.all_to_all(back, 'gy', 0, 0, tiled=True)  21.7 us
    all_to_all x1, blocking collectives, per_device(): terms = lax.all_to_all(back, 'gx', 0, 0, tiled=True)  12.3 us
    unnamed x38, local copies, waits for them, and re-layouts  9.01 us
    pallas_call x1, Pallas kernels, per_device(): call(x_local_kernel, (shape(SX, NP + 8, LANES), shape(CX, NP, CY * LANES)...  4.66 us
    pallas_call x1, Pallas kernels, per_device(): call(prepare_kernel, prep_shapes + prepared_shapes(CX, 3, 7) + prepared_s...  4.56 us
    all_to_all x1, starting transfers between devices, per_device(): got = lax.all_to_all(sent, 'gx', 0, 0, tiled=True)  4.3 us
    pallas_call x1, Pallas kernels, per_device(): call(y_owner_kernel, shape(SY, 32, LANES), 5, [pltpu.VMEM((SY, 32, LANES)...  2.79 us
  transfers between devices with their start and end apart: 1, of which 0 were waited for; matrix products, arithmetic and copies ran while one was open for 0% of the time, Pallas kernels for 5%

profile of v3, /device:TPU:32, one launch (start us, length us, event | category | flops | bytes accessed | tf_op | source)
XLA Modules:
  0.0 94.0 jit_solution(8336116045027810258)
XLA Ops:
  0.0 4.7 %shard_map.118 = (f32[8,72,128]{2,1,0:T(8,128)}, f32[8,64,512]{2,1,0:T(8,128)S(1)}, f32[384,256]{1,0:T(8,128)S(1)}, f32[3,64,64]{2,1,0:T(8,128)S(1)}, s32[4,128]...) custom-call(s32[1]{0:T(128)} %bitcast.rank_ref, f32[64,32,128]{2,1,0:T(8,128)} %bitcast.11, ...), custom_call_target="tpu_custom_call" | custom-call | tf_op jit(solution)/shard_map/pallas_call | solution.py:673
  4.7 0.6 copy-done.11
  5.3 0.0 copy-done.17
  5.3 4.3 %all-to-all-start = ((f32[8,72,128]{2,1,0:T(8,128)}), f32[8,72,128]{2,1,0:T(8,128)S(1)}, u32[]{:S(2)}, u32[]{:S(2)}) async-start(f32[8,72,128]{2,1,0:T(8,128)} %get-tuple-element.33), calls=%async_computation | async-start | bytes 589824 | tf_op jit(solution)/shard_map/all_to_all | solution.py:695
  9.6 4.6 %shard_map.119 = (bf16[384,256]{1,0:T(8,128)(2,1)S(1)}, bf16[576,256]{1,0:T(8,128)(2,1)S(1)}, bf16[704,256]{1,0:T(8,128)(2,1)S(1)}, bf16[704,256]{1,0:T(8,128)(2...) custom-call(f32[384,256]{1,0:T(8,128)S(1)} %get-tuple-element.28.mat, ...), custom_call_target="tpu_custom_call" | custom-call | tf_op jit(solution)/shard_map/pallas_call | solution.py:697
  14.1 0.7 copy-done
  14.8 0.7 copy-done.2
  15.5 0.7 copy-done.4
  16.2 0.7 copy-done.7
  16.8 0.6 copy-done.9
  17.5 0.6 copy-done.13
  18.1 0.6 copy-done.15
  18.7 0.7 copy-done.16
  19.3 0.9 copy-done.1
  20.3 0.9 copy-done.3
  21.2 1.2 %shard_map.120 = f32[8,64,128]{2,1,0:T(8,128)S(1)} custom-call(f32[8,72,128]{2,1,0:T(8,128)S(1)} %all-to-all-done.in_ref, bf16[704,256]{1,0:T(8,128)(2,1)S(1)} %get-tuple-element.34.gain_ref, bf16[448,256]{1,0:T(8,128)(2,1)S(1)} %copy-done.1, bf16[448,256]{1,0:T(8,128)(2,1)S(1)} %copy-done.3, f32[8,128]{1,0:T(8,128)S(1)} %copy-done.16), custom_call_target="tpu_custom_call" | custom-call | tf_op jit(solution)/shard_map/pallas_call | solution.py:703
  22.5 12.3 %all_to_all.20.in_ref = f32[8,64,128]{2,1,0:T(8,128)S(1)} all-to-all(f32[8,64,128]{2,1,0:T(8,128)S(1)} %shard_map.120), channel_id=1, replica_groups=mesh['gx'=8,'gy'=32] {'gx'}, dimensions={0} | all-to-all | bytes 524288 | tf_op jit(solution)/shard_map/all_to_all | solution.py:704
  34.8 0.7 copy-done.12
  35.4 2.1 %shard_map.121 = (f32[4,64,1024]{2,1,0:T(8,128)S(1)}, f32[1088,128]{1,0:T(8,128)S(1)}) custom-call(s32[1]{0:T(128)} %bitcast.rank_ref, f32[8,64,512]{2,1,0:T(8,128)S(1)} %get-tuple-element.26.local_ref, f32[3,32,128]{2,1,0:T(8,128)S(1)} %bitcast.10, s32[4,128]{1,0:T(4,128)S(1)} %copy-done.18, bf16[384,256]{1,0:T(8,128)(2,1)S(1)} %copy-done.5, ...), custom_call_target="tpu_custom_call" | custom-call | tf_op jit(solution)/shard_map/pallas_call | solution.py:705
  37.6 29.2 %all_to_all.21 = f32[32,17,2,128]{3,2,1,0:T(2,128)S(1)} all-to-all(f32[32,17,2,128]{3,2,1,0:T(2,128)S(1)} %bitcast.8), channel_id=1, replica_groups=mesh['gx'=8,'gy'=32] {'gy'}, dimensions={0} | all-to-all | bytes 1114112 | tf_op jit(solution)/shard_map/all_to_all | solution.py:712
  66.8 0.7 copy-done.14
  67.5 2.8 %shard_map.122 = f32[32,32,128]{2,1,0:T(8,128)S(1)} custom-call(f32[1088,128]{1,0:T(8,128)S(1)} %bitcast.7, bf16[256,256]{1,0:T(8,128)(2,1)S(1)} %copy-done.8, bf16[640,256]{1,0:T(8,128)(2,1)S(1)} %get-tuple-element.44.up_ref, bf16[640,256]{1,0:T(8,128)(2,1)S(1)} %get-tuple-element.45.down_ref, f32[8,128]{1,0:T(8,128)S(1)} %copy-done.14), custom_call_target="tpu_custom_call" | custom-call | tf_op jit(solution)/shard_map/pallas_call | solution.py:713
  70.3 21.7 %all_to_all.22.in_ref = f32[32,32,128]{2,1,0:T(8,128)S(1)} all-to-all(f32[32,32,128]{2,1,0:T(8,128)S(1)} %shard_map.122), channel_id=1, replica_groups=mesh['gx'=8,'gy'=32] {'gy'}, dimensions={0} | all-to-all | bytes 1048576 | tf_op jit(solution)/shard_map/all_to_all | solution.py:716
  92.0 2.1 %shard_map.123 = f32[64,32,128]{2,1,0:T(8,128)} custom-call(f32[4,64,1024]{2,1,0:T(8,128)S(1)} %get-tuple-element.40.local_ref, f32[3,32,128]{2,1,0:T(8,128)S(1)} %get-tuple-element.38.coef_y_ref, s32[8,128]{1,0:T(8,128)S(1)} %copy-done.12, bf16[576,256]{1,0:T(8,128)(2,1)S(1)} %get-tuple-element.31.parts_y_ref.parts_ref, bf16[256,256]{1,0:T(8,128)(2,1)S(1)} %copy-done.10, ...), custom_call_target="tpu_custom_call" | custom-call | tf_op jit(solution)/shard_map/pallas_call | solution.py:717
  (25 shorter events, 0.1 us)
Async XLA Ops:
  4.7 0.6 copy-start.11
  4.7 0.6 copy-start.17
  5.3 13.4 %all-to-all-start = ((f32[8,72,128]{2,1,0:T(8,128)}), f32[8,72,128]{2,1,0:T(8,128)S(1)}, u32[]{:S(2)}, u32[]{:S(2)}) async-start(f32[8,72,128]{2,1,0:T(8,128)} %get-tuple-element.33), calls=%async_computation | async-start | bytes 589824 | tf_op jit(solution)/shard_map/all_to_all | solution.py:695
  14.1 0.7 copy-start
  14.8 0.7 copy-start.2
  15.5 0.7 copy-start.4
  16.2 0.7 copy-start.7
  16.8 0.6 copy-start.9
  17.5 0.6 copy-start.13
  18.1 0.6 copy-start.15
  18.7 0.7 copy-start.16
  19.3 0.9 copy-start.1
  20.3 0.9 copy-start.3
  22.5 12.3 %copy-start.5 = (bf16[384,256]{1,0:T(8,128)(2,1)S(1)}, bf16[384,256]{1,0:T(8,128)(2,1)}, u32[]{:S(2)}) copy-start(bf16[384,256]{1,0:T(8,128)(2,1)} %copy-done.4) | copy-start | bytes 589828
  22.5 12.3 %copy-start.6 = (f32[3,8,4,128]{3,2,1,0:T(4,128)S(1)}, f32[3,8,4,128]{3,2,1,0:T(4,128)}, u32[]{:S(2)}) copy-start(f32[3,8,4,128]{3,2,1,0:T(4,128)} %param.13) | copy-start | bytes 147460
  34.8 0.7 copy-start.12
  34.8 0.7 copy-start.18
  37.6 29.2 %copy-start.8 = (bf16[256,256]{1,0:T(8,128)(2,1)S(1)}, bf16[256,256]{1,0:T(8,128)(2,1)}, u32[]{:S(2)}) copy-start(bf16[256,256]{1,0:T(8,128)(2,1)} %copy-done.7) | copy-start | bytes 393220
  66.8 0.7 copy-start.14
  70.3 21.7 %copy-start.10 = (bf16[256,256]{1,0:T(8,128)(2,1)S(1)}, bf16[256,256]{1,0:T(8,128)(2,1)}, u32[]{:S(2)}) copy-start(bf16[256,256]{1,0:T(8,128)(2,1)} %copy-done.9) | copy-start | bytes 393220

commit v4 on v3

--- a/solution.py
+++ b/solution.py
@@ -142,53 +142,110 @@
     return stack
 
 
-def prepare(cells, far, up, down, scale, bounds, gain_ref, from_ref, up_ref, down_ref, norm_ref):
+def prepare(cells, far, up, down, scale, bounds, gain_ref, from_ref, up_ref, down_ref, done):
     halves = cells.bit_length() - 1
     ups = [up]
     for _ in range(halves):
         ups.append(multiply(ups[-1], ups[-1]))
     scaled = scale
     for k in range(halves):
-        scaled = jnp.concatenate([scaled, multiply(scaled, ups[k])], axis=0)
+        scaled = jnp.concatenate([scaled, apply(split_matrix(scaled), ups[k])], axis=0)
+    from_ref[0 : cells * NP, :] = split_matrix(scaled)
+    if bounds is not None:
+        for k in range(halves):
+            bounds = apply(split_matrix(bounds), ups[k])
+        from_ref[cells * NP :, :] = split_matrix(bounds)
+    done(from_ref)
     downs = powers_of(down, cells)
     stack = split_matrix(downs)
-    from_ref[0 : cells * NP, :] = split_matrix(scaled)
     for j in range(cells):
         gain = apply(block(stack, j), block(scaled, j))
         gain_ref[NP * j : NP * (j + 1), :] = split_matrix(gain)
     if bounds is not None:
-        for k in range(halves):
-            bounds = multiply(bounds, ups[k])
-        from_ref[cells * NP :, :] = split_matrix(bounds)
         for kind in range(3):
             gain = apply(block(stack, cells - 1), block(bounds, kind))
             gain_ref[NP * (cells + kind) : NP * (cells + kind + 1), :] = split_matrix(gain)
-    norm_ref[...] = jnp.zeros(norm_ref.shape, F32)
+    done(gain_ref)
     tops = ((ups[halves], up_ref), (block(downs, cells - 1), down_ref))
-    for row, (power, ref) in enumerate(tops):
+    for power, ref in tops:
         norm = jnp.max(jnp.sum(jnp.abs(power[:, :NP]), axis=1, keepdims=True), axis=0, keepdims=True)
         norm = jnp.maximum(norm, 1e-30)
-        norm_ref[row : row + 1, :] = jnp.broadcast_to(norm, (1, LANES))
+        count = ref.shape[0] // NP
+        ref[count * NP :, :] = split_matrix(jnp.broadcast_to(norm, (16, 4 * NP)))
         near = powers_of(power / norm, 7)
         ref[0 : 7 * NP, :] = split_matrix(near)
         if far:
             power8 = multiply(block(near, 3), block(near, 3))
             power16 = multiply(power8, power8)
             power24 = multiply(power16, power8)
-            ref[7 * NP :, :] = split_matrix(jnp.concatenate([power8, power16, power24], axis=0))
+            ref[7 * NP : 10 * NP, :] = split_matrix(
+                jnp.concatenate([power8, power16, power24], axis=0)
+            )
+        done(ref)
     return ups, scaled, stack
 
 
-def prepare_kernel(mats_ref, raw_ref, parts_ref, parts_y_ref, *outs):
+def norm_of(ref):
+    parts = ref[ref.shape[0] - 16 :, :].astype(F32)[0:1]
+    return parts[:, 0:1] + parts[:, NP : NP + 1] + parts[:, 3 * NP : 3 * NP + 1]
+
+
+def prepare_kernel(
+    mats_ref,
+    raw_ref,
+    gain_ref,
+    up_ref,
+    down_ref,
+    from_hbm,
+    parts_hbm,
+    parts_y_hbm,
+    gain_y_hbm,
+    from_y_hbm,
+    up_y_hbm,
+    down_y_hbm,
+    from_ref,
+    parts_ref,
+    parts_y_ref,
+    gain_y_ref,
+    from_y_ref,
+    up_y_ref,
+    down_y_ref,
+    sems,
+):
+    targets = (
+        (from_ref, from_hbm),
+        (parts_ref, parts_hbm),
+        (parts_y_ref, parts_y_hbm),
+        (gain_y_ref, gain_y_hbm),
+        (from_y_ref, from_y_hbm),
+        (up_y_ref, up_y_hbm),
+        (down_y_ref, down_y_hbm),
+    )
+    sends = []
+
+    def done(ref):
+        for k, (source, target) in enumerate(targets):
+            if source is ref:
+                sends.append(pltpu.make_async_copy(source, target, sems.at[k]))
+                sends[-1].start()
+
     ux, wx, b0, b1, b2, dx = [mats_ref[NP * k : NP * (k + 1), :] for k in range(6)]
     bounds = jnp.concatenate([b0, b1, b2], axis=0)
-    _, _, stack = prepare(CX, False, ux, dx, wx, bounds, *outs[:5])
+    _, _, stack = prepare(
+        CX, False, ux, dx, wx, bounds, gain_ref, from_ref, up_ref, down_ref, done
+    )
     parts_ref[...] = stack[: 6 * NP]
+    done(parts_ref)
     uy, wy, dy = [tiled(raw_ref[k]) for k in range(3)]
-    ups, scaled, stack = prepare(CY, True, uy, dy, wy, None, *outs[5:])
+    ups, scaled, stack = prepare(
+        CY, True, uy, dy, wy, None, gain_y_ref, from_y_ref, up_y_ref, down_y_ref, done
+    )
     extra = [uy, scaled[: 3 * NP], multiply(ups[1], uy)]
     parts_y_ref[0 : 5 * NP, :] = split_matrix(jnp.concatenate(extra, axis=0))
     parts_y_ref[5 * NP :, :] = stack
+    done(parts_y_ref)
+    for copy in sends:
+        copy.wait()
 
 
 def x_rates(coef_ref, which, i):
@@ -207,17 +264,15 @@
     uy,
     wy,
     dy,
-    coef_y_hbm,
     order_hbm,
     out_ref,
     scaled_ref,
     mats_ref,
     raw_y_ref,
-    flags_ref,
-    coef_y_ref,
-    order_ref,
     rhs_ref,
     coef_ref,
+    flags_ref,
+    order_ref,
     raw_ref,
     bounds_ref,
     sems,
@@ -228,8 +283,8 @@
     for k in range(PIECES):
         sources.append(rhs_hbm.at[:, 8 * k : 8 * (k + 1), :])
         targets.append(rhs_ref.at[k])
-    sources += [uy, wy, dy, coef_y_hbm, order_hbm]
-    targets += [raw_y_ref.at[0], raw_y_ref.at[1], raw_y_ref.at[2], coef_y_ref, order_ref]
+    sources += [uy, wy, dy, order_hbm]
+    targets += [raw_y_ref.at[0], raw_y_ref.at[1], raw_y_ref.at[2], order_ref]
     copies = []
     for k, (source, target) in enumerate(zip(sources, targets)):
         copies.append(pltpu.make_async_copy(source, target, sems.at[k]))
@@ -310,6 +365,8 @@
     g = row_of(downs[0]) * apply(down, g)
     for copy in copies[6 + PIECES :]:
         copy.wait()
+    scaled_ref[CX, 0:CY, 0:LANES] = flags_ref[...].astype(F32)
+    scaled_ref[CX, 8 : 8 + CX, 0:LANES] = order_ref[...].astype(F32)
     for y, (fy, gy) in enumerate(zip(columns(f), columns(g))):
         even, odd = regroup([fy, gy], NP)
         out_ref[2 * y, 0:NP, :] = even
@@ -336,7 +393,7 @@
             out_ref[2 * y + 1, NP + r : NP + r + 1, :] = odd[y : y + 1]
 
 
-def x_owner_kernel(in_ref, gain_ref, up_ref, down_ref, norm_ref, out_ref):
+def x_owner_kernel(in_ref, gain_ref, up_ref, down_ref, out_ref):
     half = SX // 2
     fs, gs, sa, sb = [], [], [], []
     for j in range(half):
@@ -351,8 +408,8 @@
     odd = jnp.concatenate(sb, axis=1)
     scalar = [(even if k % 2 == 0 else odd)[k // 2 : k // 2 + 1] for k in range(13)]
     width, ncol = NP, half
-    up_rate = scalar[0] * norm_ref[0:1, 0:1]
-    down_rate = scalar[1] * norm_ref[1:2, 0:1]
+    up_rate = scalar[0] * norm_of(up_ref)
+    down_rate = scalar[1] * norm_of(down_ref)
     h = scan_segments(
         shifted(f, 1, width, ncol, False),
         shifted(up_rate, 1, width, ncol, False),
@@ -398,13 +455,11 @@
     rank_ref,
     local_ref,
     coef_ref,
-    flags_ref,
     parts_ref,
     parts_y_ref,
     from_ref,
     in_ref,
     coef_y_ref,
-    order_ref,
     scaled_ref,
     out_ref,
     adj_ref,
@@ -422,7 +477,6 @@
         hs.append(h)
         es.append(e)
     through = apply(from_ref[...], jnp.concatenate(hs, axis=1))
-    flags = row_of(flags_ref[...])
     up_rates = [jnp.ones((CY, LANES), F32)]
     for i in range(CX - 1):
         up_rates.append(up_rates[-1] * x_rates(coef_ref, 1, i))
@@ -442,10 +496,14 @@
         for y in range(CY):
             adj_ref[y, :, LANES * i : LANES * (i + 1)] = g[:, LANES * y : LANES * (y + 1)]
 
-    s = [scaled(i) for i in range(CX)]
-    s[7] = s[7] + jnp.concatenate(es, axis=1)
+    s = [scaled(i) for i in range(CX - 1)]
+    pair = [
+        s[2 * k] + row_of(downs[2 * k + 1]) * apply(block(down, 0), s[2 * k + 1]) for k in range(3)
+    ]
+    flags = row_of(local_ref[CX, 0:CY, 0:LANES])
+    s.append(scaled(CX - 1) + jnp.concatenate(es, axis=1))
     keep(7, s[7])
-    pair = [s[2 * k] + row_of(downs[2 * k + 1]) * apply(block(down, 0), s[2 * k + 1]) for k in range(4)]
+    pair.append(s[6] + row_of(downs[7]) * apply(block(down, 0), s[7]))
     two = [downs[2 * k + 1] * downs[2 * k + 2] for k in range(3)]
     g = [pair[0], s[1], pair[1], s[3], pair[2], s[5]]
     for k in (3, 2, 1):
@@ -461,8 +519,9 @@
         keep(i, g[i])
     keep(6, pair[3])
 
-    flip = order_ref[...] > 0
-    flip_row = row_of(order_ref[...]) > 0
+    order = local_ref[CX, 8 : 8 + CX, 0:LANES]
+    flip = order > 0
+    flip_row = row_of(order) > 0
 
     def oriented(which, p):
         return y_rates(coef_y_ref, which, flip, p)
@@ -510,7 +569,7 @@
             out_ref[row + 33 : row + 34, :] = second[a][x : x + 1]
 
 
-def y_owner_kernel(in_ref, gain_ref, up_ref, down_ref, norm_ref, out_ref, res_ref):
+def y_owner_kernel(in_ref, gain_ref, up_ref, down_ref, out_ref, res_ref):
     width, ncol = 32, 8
     flip = replicate(in_ref[33:34, :], width)[2] > 0.5
 
@@ -527,8 +586,8 @@
     f = jnp.concatenate(fs, axis=1)
     g = jnp.concatenate(gs, axis=1)
     scalars = [jnp.concatenate([s[k] for s in ss], axis=1) for k in range(6)]
-    up_rate = scalars[0] * norm_ref[0:1, 0:1]
-    down_rate = scalars[1] * norm_ref[1:2, 0:1]
+    up_rate = scalars[0] * norm_of(up_ref)
+    down_rate = scalars[1] * norm_of(down_ref)
     h = scan_segments(
         shifted(f, 1, width, ncol, False),
         shifted(up_rate, 1, width, ncol, False),
@@ -613,32 +672,17 @@
     return pltpu.with_memory_space_constraint(a, pltpu.HBM)
 
 
-def shape(*dims, dtype=F32):
-    return jax.ShapeDtypeStruct(dims, dtype)
-
-
-def call(kernel, out_shape, n_in, scratch=(), scalars=0, space=pltpu.VMEM, out_space=pltpu.VMEM):
-    whole = pl.BlockSpec(memory_space=out_space)
+def call(kernel, outs, spaces, scratch=(), scalars=0):
+    shapes = tuple(space(dims, dtype) for space, dims, dtype in outs)
     specs = [pl.BlockSpec(memory_space=pltpu.SMEM)] * scalars
-    specs += [pl.BlockSpec(memory_space=space)] * n_in
-    outs = jax.tree.map(lambda _: whole, out_shape)
+    specs += [pl.BlockSpec(memory_space=s) for s in spaces]
     return pl.pallas_call(
         kernel,
-        out_shape=out_shape,
+        out_shape=shapes,
         in_specs=specs,
-        out_specs=outs,
+        out_specs=tuple(pl.BlockSpec(memory_space=out[0]) for out in outs),
         scratch_shapes=list(scratch),
         compiler_params=pltpu.CompilerParams(vmem_limit_bytes=VMEM_LIMIT),
-    )
-
-
-def prepared_shapes(cells, extra, powers):
-    return (
-        shape((cells + extra) * NP, 4 * NP, dtype=BF16),
-        shape((cells + extra) * NP, 4 * NP, dtype=BF16),
-        shape(powers * NP, 4 * NP, dtype=BF16),
-        shape(powers * NP, 4 * NP, dtype=BF16),
-        shape(8, LANES),
     )
 
 
@@ -656,74 +700,78 @@
     bc_flags,
     line_order,
 ):
+    vmem, hbm = pltpu.VMEM, pltpu.HBM
     rank = lax.axis_index("gx").astype(jnp.int32).reshape(1)
-    mats = (
-        out_coupling_x,
-        inverse_x,
-        in_coupling_x,
-        boundary_inverse,
-        out_coupling_y,
-        inverse_y,
-        in_coupling_y,
-    )
+    mats_x = (out_coupling_x, inverse_x, in_coupling_x, boundary_inverse)
+    mats_y = (out_coupling_y, inverse_y, in_coupling_y)
     rhs = rhs.reshape(NP, CX * CY, LANES)
     coef_x = coef_x.reshape(3, CX * CY, LANES)
     coef_y = coef_y.reshape(3, CX * CY, LANES)
 
-    sent, local, tiles, raw_y, flags, coef_y, order = call(
+    sent, local, tiles, raw_y = call(
         x_local_kernel,
         (
-            shape(SX, NP + 8, LANES),
-            shape(CX, NP, CY * LANES),
-            shape(6 * NP, 4 * NP),
-            shape(3, NP, NP),
-            shape(CY, LANES, dtype=jnp.int32),
-            shape(3, CX * CY, LANES),
-            shape(CX, LANES, dtype=jnp.int32),
+            (vmem, (SX, NP + 8, LANES), F32),
+            (vmem, (CX + 1, NP, CY * LANES), F32),
+            (vmem, (6 * NP, 4 * NP), F32),
+            (vmem, (3, NP, NP), F32),
         ),
-        12,
+        (hbm,) * 11,
         [
-            pltpu.VMEM((PIECES, NP, 8, LANES), F32),
-            pltpu.VMEM((3, CX * CY, LANES), F32),
-            pltpu.VMEM((3, NP, NP), F32),
-            pltpu.VMEM((3, NP, NP), F32),
-            pltpu.SemaphoreType.DMA((11 + PIECES,)),
+            vmem((PIECES, NP, 8, LANES), F32),
+            vmem((3, CX * CY, LANES), F32),
+            vmem((CY, LANES), jnp.int32),
+            vmem((CX, LANES), jnp.int32),
+            vmem((3, NP, NP), F32),
+            vmem((3, NP, NP), F32),
+            pltpu.SemaphoreType.DMA((10 + PIECES,)),
         ],
         1,
-        pltpu.HBM,
-    )(rank, *[in_hbm(a) for a in (rhs, coef_x, bc_flags) + mats + (coef_y, line_order)])
+    )(rank, *[in_hbm(a) for a in (rhs, coef_x, bc_flags) + mats_x + mats_y + (line_order,)])
     got = lax.all_to_all(sent, "gx", 0, 0, tiled=True)
-    prep_shapes = (shape(6 * NP, 4 * NP, dtype=BF16), shape(9 * NP, 4 * NP, dtype=BF16))
-    prep = call(
-        prepare_kernel, prep_shapes + prepared_shapes(CX, 3, 7) + prepared_shapes(CY, 0, 10), 2
+    later = [
+        (rows, 4 * NP)
+        for rows in (11 * NP, 6 * NP, 9 * NP, 4 * NP, 4 * NP, 10 * NP + 16, 10 * NP + 16)
+    ]
+    gain_x, up_x, down_x, from_x, parts_x, parts_y, gain_y, from_y, up_y, down_y = call(
+        prepare_kernel,
+        (
+            (vmem, (11 * NP, 4 * NP), BF16),
+            (vmem, (7 * NP + 16, 4 * NP), BF16),
+            (vmem, (7 * NP + 16, 4 * NP), BF16),
+        )
+        + tuple((hbm, dims, BF16) for dims in later),
+        (vmem, vmem),
+        [vmem(dims, BF16) for dims in later] + [pltpu.SemaphoreType.DMA((7,))],
     )(tiles, raw_y)
-    parts_x, parts_y = prep[:2]
-    gain_x, from_x, up_x, down_x, norm_x = prep[2:7]
-    gain_y, from_y, up_y, down_y, norm_y = prep[7:]
-    back = call(x_owner_kernel, shape(SX, NP, LANES), 5)(got, gain_x, up_x, down_x, norm_x)
+    (back,) = call(x_owner_kernel, ((vmem, (SX, NP, LANES), F32),), (vmem,) * 4)(
+        got, gain_x, up_x, down_x
+    )
     terms = lax.all_to_all(back, "gx", 0, 0, tiled=True)
     local, sent = call(
         middle_kernel,
-        (shape(CY, NP, CX * LANES), shape(SY * ROWS, LANES)),
-        9,
-        [pltpu.VMEM((CY, NP, CX * LANES), F32)],
+        ((vmem, (CY, NP, CX * LANES), F32), (vmem, (SY * ROWS, LANES), F32)),
+        (vmem,) * 7,
+        [vmem((CY, NP, CX * LANES), F32)],
         1,
-    )(rank, local, coef_x, flags, parts_x, parts_y, from_x, terms, coef_y, order)
+    )(rank, local, coef_x, parts_x, parts_y, from_x, terms, coef_y)
     got = lax.all_to_all(sent.reshape(SY, ROWS // 2, 2, LANES), "gy", 0, 0, tiled=True)
-    back = call(
-        y_owner_kernel, shape(SY, 32, LANES), 5, [pltpu.VMEM((SY, 32, LANES), F32)]
-    )(got.reshape(SY * ROWS, LANES), gain_y, up_y, down_y, norm_y)
+    (back,) = call(
+        y_owner_kernel,
+        ((vmem, (SY, 32, LANES), F32),),
+        (vmem,) * 4,
+        [vmem((SY, 32, LANES), F32)],
+    )(got.reshape(SY * ROWS, LANES), gain_y, up_y, down_y)
     terms = lax.all_to_all(back, "gy", 0, 0, tiled=True)
-    out = call(
+    (out,) = call(
         y_final_kernel,
-        shape(NP, CX * CY, LANES),
-        6,
+        ((hbm, (NP, CX * CY, LANES), F32),),
+        (vmem,) * 6,
         [
-            pltpu.VMEM((HALVES, NP, CX * CY // HALVES, LANES), F32),
+            vmem((HALVES, NP, CX * CY // HALVES, LANES), F32),
             pltpu.SemaphoreType.DMA((HALVES,)),
         ],
-        out_space=pltpu.HBM,
-    )(local, coef_y, order, parts_y, from_y, terms)
+    )(local, coef_y, line_order, parts_y, from_y, terms)
     return out.reshape(NP, CX, CY, LANES)
 
 

time: 94.5 us -> 86.2 us (0.912)
  local copies, waits for them, and re-layouts: 9.01 us -> 0.05 us
  waiting for transfers between devices: 0.01 us -> 2.92 us
  blocking collectives: 63.2 us -> 60.6 us
    unnamed x38 -> x20, local copies, waits for them, and re-layouts: 9.01 us -> 0.05 us
    all_to_all x1, waiting for transfers between devices: 0.01 us -> 2.92 us  [per_device(): got = lax.all_to_all(sent, 'gx', 0, 0, tiled=True)]
    all_to_all x1, blocking collectives: 12.3 us -> 9.95 us  [per_device(): terms = lax.all_to_all(back, 'gx', 0, 0, tiled=True)]
  transfers between devices with their start and end apart: 1 -> 1, of which waited for: 0 -> 1; matrix products, arithmetic and copies ran while one was open for 0% -> 0% of each run, Pallas kernels for 5% -> 6%
where the time goes in v4:
time: 86.2 us; the launch traced here: 85.9 us
  blocking collectives  60.6 us (70%)
  Pallas kernels  17.9 us (21%)
  starting transfers between devices  4.32 us (5%)
  waiting for transfers between devices  2.92 us (3%)
    all_to_all x1, blocking collectives, per_device(): lax.all_to_all(sent.reshape(SY, ROWS // 2, 2, LANES), 'gy', 0, 0, tiled=T...  29.1 us
    all_to_all x1, blocking collectives, per_device(): terms = lax.all_to_all(back, 'gy', 0, 0, tiled=True)  21.5 us
    all_to_all x1, blocking collectives, per_device(): terms = lax.all_to_all(back, 'gx', 0, 0, tiled=True)  9.95 us
    pallas_call x1, Pallas kernels, per_device(): call(prepare_kernel, ((vmem, (11 * NP, 4 * NP), BF16), (vmem, (7 * NP + 1...  4.91 us
    pallas_call x1, Pallas kernels, per_device(): call(x_local_kernel, ((vmem, (SX, NP + 8, LANES), F32), (vmem, (CX + 1, N...  4.64 us
    all_to_all x1, starting transfers between devices, per_device(): got = lax.all_to_all(sent, 'gx', 0, 0, tiled=True)  4.32 us
    all_to_all x1, waiting for transfers between devices, per_device(): got = lax.all_to_all(sent, 'gx', 0, 0, tiled=True)  2.92 us
    pallas_call x1, Pallas kernels, per_device(): call(y_owner_kernel, ((vmem, (SY, 32, LANES), F32),), (vmem,) * 4, [vmem(...  2.82 us
  transfers between devices with their start and end apart: 1, of which 1 were waited for; matrix products, arithmetic and copies ran while one was open for 0% of the time, Pallas kernels for 6%

profile of v4, /device:TPU:32, one launch (start us, length us, event | category | flops | bytes accessed | tf_op | source)
XLA Modules:
  0.0 85.9 jit_solution(13406542079060834046)
XLA Ops:
  0.0 4.6 %shard_map.118 = (f32[8,72,128]{2,1,0:T(8,128)}, f32[9,64,512]{2,1,0:T(8,128)S(1)}, f32[384,256]{1,0:T(8,128)S(1)}, f32[3,64,64]{2,1,0:T(8,128)S(1)}) custom-call(s32[1]{0:T(128)} %bitcast.rank_ref, f32[64,32,128]{2,1,0:T(8,128)} %bitcast.13, f32[3,32,128]{2,1,0:T(8,128)} %bitcast.9, s32[4,128]{1,0:T(4,128)} %flags_hbm.1, f32[64,64]{1,0:T(8,128)} %ux.1, ...), custom_call_target="tpu_custom_call" | custom-call | tf_op jit(solution)/shard_map/pallas_call | solution.py:711
  4.6 4.3 %all-to-all-start = ((f32[8,72,128]{2,1,0:T(8,128)}), f32[8,72,128]{2,1,0:T(8,128)S(1)}, u32[]{:S(2)}, u32[]{:S(2)}) async-start(f32[8,72,128]{2,1,0:T(8,128)} %get-tuple-element.27), calls=%async_computation | async-start | bytes 589824 | tf_op jit(solution)/shard_map/all_to_all | solution.py:731
  9.0 0.0 copy-start.6
  9.0 4.9 %shard_map.119 = (bf16[704,256]{1,0:T(8,128)(2,1)S(1)}, bf16[464,256]{1,0:T(8,128)(2,1)S(1)}, bf16[464,256]{1,0:T(8,128)(2,1)S(1)}, bf16[704,256]{1,0:T(8,128)(2...) custom-call(f32[384,256]{1,0:T(8,128)S(1)} %get-tuple-element.22.mat, ...), custom_call_target="tpu_custom_call" | custom-call | tf_op jit(solution)/shard_map/pallas_call | solution.py:736
  13.9 0.0 copy-start
  13.9 0.0 copy-start.1
  13.9 0.0 copy-start.4
  13.9 2.9 %all-to-all-done.in_ref = f32[8,72,128]{2,1,0:T(8,128)S(1)} async-done(((f32[8,72,128]{2,1,0:T(8,128)}), f32[8,72,128]{2,1,0:T(8,128)S(1)}, u32[]{:S(2)}, u32[]{:S(2)}) %all-to-all-start) | async-done | bytes 294944 | tf_op jit(solution)/shard_map/all_to_all | solution.py:731
  16.9 1.3 %shard_map.120 = f32[8,64,128]{2,1,0:T(8,128)S(1)} custom-call(f32[8,72,128]{2,1,0:T(8,128)S(1)} %all-to-all-done.in_ref, bf16[704,256]{1,0:T(8,128)(2,1)S(1)} %get-tuple-element.28.gain_ref, bf16[464,256]{1,0:T(8,128)(2,1)S(1)} %get-tuple-element.29.up_ref, bf16[464,256]{1,0:T(8,128)(2,1)S(1)} %get-tuple-element.30.down_ref), custom_call_target="tpu_custom_call" | custom-call | tf_op jit(solution)/shard_map/pallas_call | solution.py:747
  18.2 9.9 %all_to_all.20.in_ref = f32[8,64,128]{2,1,0:T(8,128)S(1)} all-to-all(f32[8,64,128]{2,1,0:T(8,128)S(1)} %shard_map.120), channel_id=1, replica_groups=mesh['gx'=8,'gy'=32] {'gx'}, dimensions={0} | all-to-all | bytes 524288 | tf_op jit(solution)/shard_map/all_to_all | solution.py:750
  28.1 0.0 copy-done.5
  28.1 0.0 copy-done.6
  28.1 0.0 copy-done.1
  28.1 0.0 copy-done.4
  28.1 0.0 copy-start.2
  28.2 0.0 copy-start.3
  28.2 0.0 copy-start.7
  28.2 2.1 %shard_map.121 = (f32[4,64,1024]{2,1,0:T(8,128)S(1)}, f32[1088,128]{1,0:T(8,128)S(1)}) custom-call(s32[1]{0:T(128)} %bitcast.rank_ref, f32[9,64,512]{2,1,0:T(8,128)S(1)} %get-tuple-element.21.local_ref, f32[3,32,128]{2,1,0:T(8,128)S(1)} %bitcast.10, bf16[384,256]{1,0:T(8,128)(2,1)S(1)} %copy-done.4, bf16[576,256]{1,0:T(8,128)(2,1)S(1)} %copy-done, ...), custom_call_target="tpu_custom_call" | custom-call | tf_op jit(solution)/shard_map/pallas_call | solution.py:751
  30.3 29.1 %all_to_all.21 = f32[32,17,2,128]{3,2,1,0:T(2,128)S(1)} all-to-all(f32[32,17,2,128]{3,2,1,0:T(2,128)S(1)} %bitcast.8), channel_id=1, replica_groups=mesh['gx'=8,'gy'=32] {'gy'}, dimensions={0} | all-to-all | bytes 1114112 | tf_op jit(solution)/shard_map/all_to_all | solution.py:758
  59.4 0.0 copy-start.8
  59.4 0.0 copy-start.9
  59.4 2.8 %shard_map.122 = f32[32,32,128]{2,1,0:T(8,128)S(1)} custom-call(f32[1088,128]{1,0:T(8,128)S(1)} %bitcast.7, bf16[256,256]{1,0:T(8,128)(2,1)S(1)} %copy-done.7, bf16[656,256]{1,0:T(8,128)(2,1)S(1)} %copy-done.2, bf16[656,256]{1,0:T(8,128)(2,1)S(1)} %copy-done.3), custom_call_target="tpu_custom_call" | custom-call | tf_op jit(solution)/shard_map/pallas_call | solution.py:759
  62.2 21.5 %all_to_all.22.in_ref = f32[32,32,128]{2,1,0:T(8,128)S(1)} all-to-all(f32[32,32,128]{2,1,0:T(8,128)S(1)} %shard_map.122), channel_id=1, replica_groups=mesh['gx'=8,'gy'=32] {'gy'}, dimensions={0} | all-to-all | bytes 1048576 | tf_op jit(solution)/shard_map/all_to_all | solution.py:765
  83.8 2.1 %shard_map.123 = f32[64,32,128]{2,1,0:T(8,128)} custom-call(f32[4,64,1024]{2,1,0:T(8,128)S(1)} %get-tuple-element.31.local_ref, f32[3,32,128]{2,1,0:T(8,128)S(1)} %bitcast.12, s32[8,128]{1,0:T(8,128)S(1)} %copy-done.9, bf16[576,256]{1,0:T(8,128)(2,1)S(1)} %copy-done, bf16[256,256]{1,0:T(8,128)(2,1)S(1)} %copy-done.8, f32[32,32,128]{2,1,0:T(8,128)S(1)} %all_to_all.22.in_ref), custom_call_target="tpu_custom_call" | custom-call | tf_op jit(solution)/shard_map/pallas_call | solution.py:766
  (7 shorter events, 0.0 us)
Async XLA Ops:
  4.6 12.2 %all-to-all-start = ((f32[8,72,128]{2,1,0:T(8,128)}), f32[8,72,128]{2,1,0:T(8,128)S(1)}, u32[]{:S(2)}, u32[]{:S(2)}) async-start(f32[8,72,128]{2,1,0:T(8,128)} %get-tuple-element.27), calls=%async_computation | async-start | bytes 589824 | tf_op jit(solution)/shard_map/all_to_all | solution.py:731
  9.0 19.2 %copy-start.5 = (f32[3,8,4,128]{3,2,1,0:T(4,128)S(1)}, f32[3,8,4,128]{3,2,1,0:T(4,128)}, u32[]{:S(2)}) copy-start(f32[3,8,4,128]{3,2,1,0:T(4,128)} %param.13) | copy-start | bytes 147460
  9.0 19.2 %copy-start.6 = (f32[3,8,4,128]{3,2,1,0:T(4,128)S(1)}, f32[3,8,4,128]{3,2,1,0:T(4,128)}, u32[]{:S(2)}) copy-start(f32[3,8,4,128]{3,2,1,0:T(4,128)} %param.14) | copy-start | bytes 147460
  13.9 14.2 %copy-start = (bf16[576,256]{1,0:T(8,128)(2,1)S(1)}, bf16[576,256]{1,0:T(8,128)(2,1)}, u32[]{:S(2)}) copy-start(bf16[576,256]{1,0:T(8,128)(2,1)} %get-tuple-element.25.parts_y_ref.parts_ref) | copy-start | bytes 884740
  13.9 14.2 %copy-start.1 = (bf16[704,256]{1,0:T(8,128)(2,1)S(1)}, bf16[704,256]{1,0:T(8,128)(2,1)}, u32[]{:S(2)}) copy-start(bf16[704,256]{1,0:T(8,128)(2,1)} %get-tuple-element.26.from_ref) | copy-start | bytes 1081348
  13.9 14.2 %copy-start.4 = (bf16[384,256]{1,0:T(8,128)(2,1)S(1)}, bf16[384,256]{1,0:T(8,128)(2,1)}, u32[]{:S(2)}) copy-start(bf16[384,256]{1,0:T(8,128)(2,1)} %get-tuple-element.24.parts_ref) | copy-start | bytes 589828
  28.1 31.2 %copy-start.2 = (bf16[656,256]{1,0:T(8,128)(2,1)S(1)}, bf16[656,256]{1,0:T(8,128)(2,1)}, u32[]{:S(2)}) copy-start(bf16[656,256]{1,0:T(8,128)(2,1)} %get-tuple-element.35.up_ref) | copy-start | bytes 1007620
  28.2 31.2 %copy-start.3 = (bf16[656,256]{1,0:T(8,128)(2,1)S(1)}, bf16[656,256]{1,0:T(8,128)(2,1)}, u32[]{:S(2)}) copy-start(bf16[656,256]{1,0:T(8,128)(2,1)} %get-tuple-element.36.down_ref) | copy-start | bytes 1007620
  28.2 31.2 %copy-start.7 = (bf16[256,256]{1,0:T(8,128)(2,1)S(1)}, bf16[256,256]{1,0:T(8,128)(2,1)}, u32[]{:S(2)}) copy-start(bf16[256,256]{1,0:T(8,128)(2,1)} %get-tuple-element.34.gain_ref) | copy-start | bytes 393220
  59.4 24.4 %copy-start.8 = (bf16[256,256]{1,0:T(8,128)(2,1)S(1)}, bf16[256,256]{1,0:T(8,128)(2,1)}, u32[]{:S(2)}) copy-start(bf16[256,256]{1,0:T(8,128)(2,1)} %get-tuple-element.32.from_ref) | copy-start | bytes 393220
  59.4 24.4 %copy-start.9 = (s32[8,128]{1,0:T(8,128)S(1)}, s32[8,128]{1,0:T(8,128)}, u32[]{:S(2)}) copy-start(s32[8,128]{1,0:T(8,128)} %order_ref.1) | copy-start | bytes 12292

commit v5 on v4

--- a/solution.py
+++ b/solution.py
@@ -288,7 +288,8 @@
     copies = []
     for k, (source, target) in enumerate(zip(sources, targets)):
         copies.append(pltpu.make_async_copy(source, target, sems.at[k]))
-        copies[-1].start()
+    for k in range(len(copies)):
+        copies[k].start()
     for copy in copies[:6]:
         copy.wait()
 
@@ -310,6 +311,8 @@
     u2 = split_matrix(u2)
     d2 = multiply(d, d)
     down24 = split_matrix(jnp.concatenate([d2, multiply(d2, d2)], axis=0))
+    for copy in copies[6:]:
+        copy.wait()
     planes = rhs_ref.reshape(PIECES * NP * 8, LANES)
 
     ups = [x_rates(coef_ref, 1, i) for i in range(CX)]
@@ -335,7 +338,6 @@
 
     s, v, part = [None] * CX, [], []
     for k in range(PIECES):
-        copies[6 + k].wait()
         out = apply(end_stack if k == 0 else up_scale, given(2 * k))
         v.append(given(2 * k + 1) + row_of(ups[2 * k]) * block(out, 0))
         part.append(at_end(0, out) if k == 0 else block(out, 1))
@@ -363,8 +365,6 @@
     second = pair[2] + row_of(two[2]) * apply(down24[:NP], pair[3])
     g = first + row_of(two[0] * two[1]) * apply(down24[NP:], second)
     g = row_of(downs[0]) * apply(down, g)
-    for copy in copies[6 + PIECES :]:
-        copy.wait()
     scaled_ref[CX, 0:CY, 0:LANES] = flags_ref[...].astype(F32)
     scaled_ref[CX, 8 : 8 + CX, 0:LANES] = order_ref[...].astype(F32)
     for y, (fy, gy) in enumerate(zip(columns(f), columns(g))):

time: 86.2 us -> 85.6 us (level)
  no operation moved by 1% of the time
where the time goes in v5:
time: 85.6 us; the launch traced here: 85.3 us
  blocking collectives  60.6 us (71%)
  Pallas kernels  17.2 us (20%)
  starting transfers between devices  4.31 us (5%)
  waiting for transfers between devices  2.92 us (3%)
    all_to_all x1, blocking collectives, per_device(): lax.all_to_all(sent.reshape(SY, ROWS // 2, 2, LANES), 'gy', 0, 0, tiled=T...  29.1 us
    all_to_all x1, blocking collectives, per_device(): terms = lax.all_to_all(back, 'gy', 0, 0, tiled=True)  21.6 us
    all_to_all x1, blocking collectives, per_device(): terms = lax.all_to_all(back, 'gx', 0, 0, tiled=True)  9.95 us
    pallas_call x1, Pallas kernels, per_device(): call(prepare_kernel, ((vmem, (11 * NP, 4 * NP), BF16), (vmem, (7 * NP + 1...  4.92 us
    all_to_all x1, starting transfers between devices, per_device(): got = lax.all_to_all(sent, 'gx', 0, 0, tiled=True)  4.31 us
    pallas_call x1, Pallas kernels, per_device(): call(x_local_kernel, ((vmem, (SX, NP + 8, LANES), F32), (vmem, (CX + 1, N...  4.03 us
    all_to_all x1, waiting for transfers between devices, per_device(): got = lax.all_to_all(sent, 'gx', 0, 0, tiled=True)  2.92 us
    pallas_call x1, Pallas kernels, per_device(): call(y_owner_kernel, ((vmem, (SY, 32, LANES), F32),), (vmem,) * 4, [vmem(...  2.82 us
  transfers between devices with their start and end apart: 1, of which 1 were waited for; matrix products, arithmetic and copies ran while one was open for 0% of the time, Pallas kernels for 6%

profile of v5, /device:TPU:32, one launch (start us, length us, event | category | flops | bytes accessed | tf_op | source)
XLA Modules:
  0.0 85.3 jit_solution(1850484961765033980)
XLA Ops:
  0.0 4.0 %shard_map.118 = (f32[8,72,128]{2,1,0:T(8,128)}, f32[9,64,512]{2,1,0:T(8,128)S(1)}, f32[384,256]{1,0:T(8,128)S(1)}, f32[3,64,64]{2,1,0:T(8,128)S(1)}) custom-call(s32[1]{0:T(128)} %bitcast.rank_ref, f32[64,32,128]{2,1,0:T(8,128)} %bitcast.13, f32[3,32,128]{2,1,0:T(8,128)} %bitcast.9, s32[4,128]{1,0:T(4,128)} %flags_hbm.1, f32[64,64]{1,0:T(8,128)} %ux.1, ...), custom_call_target="tpu_custom_call" | custom-call | tf_op jit(solution)/shard_map/pallas_call | solution.py:711
  4.0 4.3 %all-to-all-start = ((f32[8,72,128]{2,1,0:T(8,128)}), f32[8,72,128]{2,1,0:T(8,128)S(1)}, u32[]{:S(2)}, u32[]{:S(2)}) async-start(f32[8,72,128]{2,1,0:T(8,128)} %get-tuple-element.27), calls=%async_computation | async-start | bytes 589824 | tf_op jit(solution)/shard_map/all_to_all | solution.py:731
  8.4 0.0 copy-start.6
  8.4 4.9 %shard_map.119 = (bf16[704,256]{1,0:T(8,128)(2,1)S(1)}, bf16[464,256]{1,0:T(8,128)(2,1)S(1)}, bf16[464,256]{1,0:T(8,128)(2,1)S(1)}, bf16[704,256]{1,0:T(8,128)(2...) custom-call(f32[384,256]{1,0:T(8,128)S(1)} %get-tuple-element.22.mat, ...), custom_call_target="tpu_custom_call" | custom-call | tf_op jit(solution)/shard_map/pallas_call | solution.py:736
  13.3 0.0 copy-start
  13.3 0.0 copy-start.1
  13.3 0.0 copy-start.4
  13.3 2.9 %all-to-all-done.in_ref = f32[8,72,128]{2,1,0:T(8,128)S(1)} async-done(((f32[8,72,128]{2,1,0:T(8,128)}), f32[8,72,128]{2,1,0:T(8,128)S(1)}, u32[]{:S(2)}, u32[]{:S(2)}) %all-to-all-start) | async-done | bytes 294944 | tf_op jit(solution)/shard_map/all_to_all | solution.py:731
  16.2 1.3 %shard_map.120 = f32[8,64,128]{2,1,0:T(8,128)S(1)} custom-call(f32[8,72,128]{2,1,0:T(8,128)S(1)} %all-to-all-done.in_ref, bf16[704,256]{1,0:T(8,128)(2,1)S(1)} %get-tuple-element.28.gain_ref, bf16[464,256]{1,0:T(8,128)(2,1)S(1)} %get-tuple-element.29.up_ref, bf16[464,256]{1,0:T(8,128)(2,1)S(1)} %get-tuple-element.30.down_ref), custom_call_target="tpu_custom_call" | custom-call | tf_op jit(solution)/shard_map/pallas_call | solution.py:747
  17.6 9.9 %all_to_all.20.in_ref = f32[8,64,128]{2,1,0:T(8,128)S(1)} all-to-all(f32[8,64,128]{2,1,0:T(8,128)S(1)} %shard_map.120), channel_id=1, replica_groups=mesh['gx'=8,'gy'=32] {'gx'}, dimensions={0} | all-to-all | bytes 524288 | tf_op jit(solution)/shard_map/all_to_all | solution.py:750
  27.5 0.0 copy-done.5
  27.5 0.0 copy-done.6
  27.5 0.0 copy-done
  27.5 0.0 copy-done.1
  27.5 0.0 copy-done.4
  27.5 0.0 copy-start.2
  27.5 0.0 copy-start.3
  27.6 2.1 %shard_map.121 = (f32[4,64,1024]{2,1,0:T(8,128)S(1)}, f32[1088,128]{1,0:T(8,128)S(1)}) custom-call(s32[1]{0:T(128)} %bitcast.rank_ref, f32[9,64,512]{2,1,0:T(8,128)S(1)} %get-tuple-element.21.local_ref, f32[3,32,128]{2,1,0:T(8,128)S(1)} %bitcast.10, bf16[384,256]{1,0:T(8,128)(2,1)S(1)} %copy-done.4, bf16[576,256]{1,0:T(8,128)(2,1)S(1)} %copy-done, ...), custom_call_target="tpu_custom_call" | custom-call | tf_op jit(solution)/shard_map/pallas_call | solution.py:751
  29.7 29.1 %all_to_all.21 = f32[32,17,2,128]{3,2,1,0:T(2,128)S(1)} all-to-all(f32[32,17,2,128]{3,2,1,0:T(2,128)S(1)} %bitcast.8), channel_id=1, replica_groups=mesh['gx'=8,'gy'=32] {'gy'}, dimensions={0} | all-to-all | bytes 1114112 | tf_op jit(solution)/shard_map/all_to_all | solution.py:758
  58.8 0.0 copy-start.8
  58.8 0.0 copy-start.9
  58.8 2.8 %shard_map.122 = f32[32,32,128]{2,1,0:T(8,128)S(1)} custom-call(f32[1088,128]{1,0:T(8,128)S(1)} %bitcast.7, bf16[256,256]{1,0:T(8,128)(2,1)S(1)} %copy-done.7, bf16[656,256]{1,0:T(8,128)(2,1)S(1)} %copy-done.2, bf16[656,256]{1,0:T(8,128)(2,1)S(1)} %copy-done.3), custom_call_target="tpu_custom_call" | custom-call | tf_op jit(solution)/shard_map/pallas_call | solution.py:759
  61.6 21.6 %all_to_all.22.in_ref = f32[32,32,128]{2,1,0:T(8,128)S(1)} all-to-all(f32[32,32,128]{2,1,0:T(8,128)S(1)} %shard_map.122), channel_id=1, replica_groups=mesh['gx'=8,'gy'=32] {'gy'}, dimensions={0} | all-to-all | bytes 1048576 | tf_op jit(solution)/shard_map/all_to_all | solution.py:765
  83.2 2.1 %shard_map.123 = f32[64,32,128]{2,1,0:T(8,128)} custom-call(f32[4,64,1024]{2,1,0:T(8,128)S(1)} %get-tuple-element.31.local_ref, f32[3,32,128]{2,1,0:T(8,128)S(1)} %bitcast.12, s32[8,128]{1,0:T(8,128)S(1)} %copy-done.9, bf16[576,256]{1,0:T(8,128)(2,1)S(1)} %copy-done, bf16[256,256]{1,0:T(8,128)(2,1)S(1)} %copy-done.8, f32[32,32,128]{2,1,0:T(8,128)S(1)} %all_to_all.22.in_ref), custom_call_target="tpu_custom_call" | custom-call | tf_op jit(solution)/shard_map/pallas_call | solution.py:766
  (7 shorter events, 0.0 us)
Async XLA Ops:
  4.0 12.2 %all-to-all-start = ((f32[8,72,128]{2,1,0:T(8,128)}), f32[8,72,128]{2,1,0:T(8,128)S(1)}, u32[]{:S(2)}, u32[]{:S(2)}) async-start(f32[8,72,128]{2,1,0:T(8,128)} %get-tuple-element.27), calls=%async_computation | async-start | bytes 589824 | tf_op jit(solution)/shard_map/all_to_all | solution.py:731
  8.3 19.2 %copy-start.5 = (f32[3,8,4,128]{3,2,1,0:T(4,128)S(1)}, f32[3,8,4,128]{3,2,1,0:T(4,128)}, u32[]{:S(2)}) copy-start(f32[3,8,4,128]{3,2,1,0:T(4,128)} %param.13) | copy-start | bytes 147460
  8.4 19.2 %copy-start.6 = (f32[3,8,4,128]{3,2,1,0:T(4,128)S(1)}, f32[3,8,4,128]{3,2,1,0:T(4,128)}, u32[]{:S(2)}) copy-start(f32[3,8,4,128]{3,2,1,0:T(4,128)} %param.14) | copy-start | bytes 147460
  13.3 14.2 %copy-start = (bf16[576,256]{1,0:T(8,128)(2,1)S(1)}, bf16[576,256]{1,0:T(8,128)(2,1)}, u32[]{:S(2)}) copy-start(bf16[576,256]{1,0:T(8,128)(2,1)} %get-tuple-element.25.parts_y_ref.parts_ref) | copy-start | bytes 884740
  13.3 14.2 %copy-start.1 = (bf16[704,256]{1,0:T(8,128)(2,1)S(1)}, bf16[704,256]{1,0:T(8,128)(2,1)}, u32[]{:S(2)}) copy-start(bf16[704,256]{1,0:T(8,128)(2,1)} %get-tuple-element.26.from_ref) | copy-start | bytes 1081348
  13.3 14.2 %copy-start.4 = (bf16[384,256]{1,0:T(8,128)(2,1)S(1)}, bf16[384,256]{1,0:T(8,128)(2,1)}, u32[]{:S(2)}) copy-start(bf16[384,256]{1,0:T(8,128)(2,1)} %get-tuple-element.24.parts_ref) | copy-start | bytes 589828
  27.5 31.2 %copy-start.2 = (bf16[656,256]{1,0:T(8,128)(2,1)S(1)}, bf16[656,256]{1,0:T(8,128)(2,1)}, u32[]{:S(2)}) copy-start(bf16[656,256]{1,0:T(8,128)(2,1)} %get-tuple-element.35.up_ref) | copy-start | bytes 1007620
  27.5 31.2 %copy-start.3 = (bf16[656,256]{1,0:T(8,128)(2,1)S(1)}, bf16[656,256]{1,0:T(8,128)(2,1)}, u32[]{:S(2)}) copy-start(bf16[656,256]{1,0:T(8,128)(2,1)} %get-tuple-element.36.down_ref) | copy-start | bytes 1007620
  27.6 31.2 %copy-start.7 = (bf16[256,256]{1,0:T(8,128)(2,1)S(1)}, bf16[256,256]{1,0:T(8,128)(2,1)}, u32[]{:S(2)}) copy-start(bf16[256,256]{1,0:T(8,128)(2,1)} %get-tuple-element.34.gain_ref) | copy-start | bytes 393220
  58.8 24.4 %copy-start.8 = (bf16[256,256]{1,0:T(8,128)(2,1)S(1)}, bf16[256,256]{1,0:T(8,128)(2,1)}, u32[]{:S(2)}) copy-start(bf16[256,256]{1,0:T(8,128)(2,1)} %get-tuple-element.32.from_ref) | copy-start | bytes 393220
  58.8 24.4 %copy-start.9 = (s32[8,128]{1,0:T(8,128)S(1)}, s32[8,128]{1,0:T(8,128)}, u32[]{:S(2)}) copy-start(s32[8,128]{1,0:T(8,128)} %order_ref.1) | copy-start | bytes 12292

commit v6 on v5

--- a/solution.py
+++ b/solution.py
@@ -632,7 +632,7 @@
     term_rates = [up_rates[p] / oriented(2, p) for p in range(CY)]
     downs = [oriented(0, p) for p in range(CY)]
     part = CX // HALVES
-    copies = []
+    copies, sums = [], []
     for half in range(HALVES):
         first = part * half
         lanes = slice(LANES * first, LANES * (first + part))
@@ -648,6 +648,13 @@
         through = apply(from_ref[...], jnp.concatenate(hs, axis=1))
         s = [local_ref[p, :, lanes] + row(term_rates[p]) * block(through, p) for p in range(CY)]
         s[3] = s[3] + jnp.concatenate(es, axis=1)
+        sums.append(s)
+    for half, s in enumerate(sums):
+        first = part * half
+
+        def row(rate):
+            return row_of(rate[first : first + part])
+
         g = list(s)
         for p in (3, 2, 1):
             out = apply(down[: NP * p], s[p])

time: 85.6 us -> 85.4 us (level)
  no operation moved by 1% of the time
where the time goes in v6:
time: 85.4 us; the launch traced here: 85.1 us
  blocking collectives  60.6 us (71%)
  Pallas kernels  17.1 us (20%)
  starting transfers between devices  4.31 us (5%)
  waiting for transfers between devices  2.92 us (3%)
    all_to_all x1, blocking collectives, per_device(): lax.all_to_all(sent.reshape(SY, ROWS // 2, 2, LANES), 'gy', 0, 0, tiled=T...  29.1 us
    all_to_all x1, blocking collectives, per_device(): terms = lax.all_to_all(back, 'gy', 0, 0, tiled=True)  21.6 us
    all_to_all x1, blocking collectives, per_device(): terms = lax.all_to_all(back, 'gx', 0, 0, tiled=True)  9.95 us
    pallas_call x1, Pallas kernels, per_device(): call(prepare_kernel, ((vmem, (11 * NP, 4 * NP), BF16), (vmem, (7 * NP + 1...  4.92 us
    all_to_all x1, starting transfers between devices, per_device(): got = lax.all_to_all(sent, 'gx', 0, 0, tiled=True)  4.31 us
    pallas_call x1, Pallas kernels, per_device(): call(x_local_kernel, ((vmem, (SX, NP + 8, LANES), F32), (vmem, (CX + 1, N...  4.03 us
    all_to_all x1, waiting for transfers between devices, per_device(): got = lax.all_to_all(sent, 'gx', 0, 0, tiled=True)  2.92 us
    pallas_call x1, Pallas kernels, per_device(): call(y_owner_kernel, ((vmem, (SY, 32, LANES), F32),), (vmem,) * 4, [vmem(...  2.82 us
  transfers between devices with their start and end apart: 1, of which 1 were waited for; matrix products, arithmetic and copies ran while one was open for 0% of the time, Pallas kernels for 6%

profile of v6, /device:TPU:32, one launch (start us, length us, event | category | flops | bytes accessed | tf_op | source)
XLA Modules:
  0.0 85.1 jit_solution(4537293543137720570)
XLA Ops:
  0.0 4.0 %shard_map.118 = (f32[8,72,128]{2,1,0:T(8,128)}, f32[9,64,512]{2,1,0:T(8,128)S(1)}, f32[384,256]{1,0:T(8,128)S(1)}, f32[3,64,64]{2,1,0:T(8,128)S(1)}) custom-call(s32[1]{0:T(128)} %bitcast.rank_ref, f32[64,32,128]{2,1,0:T(8,128)} %bitcast.13, f32[3,32,128]{2,1,0:T(8,128)} %bitcast.9, s32[4,128]{1,0:T(4,128)} %flags_hbm.1, f32[64,64]{1,0:T(8,128)} %ux.1, ...), custom_call_target="tpu_custom_call" | custom-call | tf_op jit(solution)/shard_map/pallas_call | solution.py:718
  4.0 4.3 %all-to-all-start = ((f32[8,72,128]{2,1,0:T(8,128)}), f32[8,72,128]{2,1,0:T(8,128)S(1)}, u32[]{:S(2)}, u32[]{:S(2)}) async-start(f32[8,72,128]{2,1,0:T(8,128)} %get-tuple-element.27), calls=%async_computation | async-start | bytes 589824 | tf_op jit(solution)/shard_map/all_to_all | solution.py:738
  8.4 0.0 copy-start.6
  8.4 4.9 %shard_map.119 = (bf16[704,256]{1,0:T(8,128)(2,1)S(1)}, bf16[464,256]{1,0:T(8,128)(2,1)S(1)}, bf16[464,256]{1,0:T(8,128)(2,1)S(1)}, bf16[704,256]{1,0:T(8,128)(2...) custom-call(f32[384,256]{1,0:T(8,128)S(1)} %get-tuple-element.22.mat, ...), custom_call_target="tpu_custom_call" | custom-call | tf_op jit(solution)/shard_map/pallas_call | solution.py:743
  13.3 0.0 copy-start
  13.3 0.0 copy-start.1
  13.3 0.0 copy-start.4
  13.3 2.9 %all-to-all-done.in_ref = f32[8,72,128]{2,1,0:T(8,128)S(1)} async-done(((f32[8,72,128]{2,1,0:T(8,128)}), f32[8,72,128]{2,1,0:T(8,128)S(1)}, u32[]{:S(2)}, u32[]{:S(2)}) %all-to-all-start) | async-done | bytes 294944 | tf_op jit(solution)/shard_map/all_to_all | solution.py:738
  16.2 1.3 %shard_map.120 = f32[8,64,128]{2,1,0:T(8,128)S(1)} custom-call(f32[8,72,128]{2,1,0:T(8,128)S(1)} %all-to-all-done.in_ref, bf16[704,256]{1,0:T(8,128)(2,1)S(1)} %get-tuple-element.28.gain_ref, bf16[464,256]{1,0:T(8,128)(2,1)S(1)} %get-tuple-element.29.up_ref, bf16[464,256]{1,0:T(8,128)(2,1)S(1)} %get-tuple-element.30.down_ref), custom_call_target="tpu_custom_call" | custom-call | tf_op jit(solution)/shard_map/pallas_call | solution.py:754
  17.6 9.9 %all_to_all.20.in_ref = f32[8,64,128]{2,1,0:T(8,128)S(1)} all-to-all(f32[8,64,128]{2,1,0:T(8,128)S(1)} %shard_map.120), channel_id=1, replica_groups=mesh['gx'=8,'gy'=32] {'gx'}, dimensions={0} | all-to-all | bytes 524288 | tf_op jit(solution)/shard_map/all_to_all | solution.py:757
  27.5 0.0 copy-done.5
  27.5 0.0 copy-done.6
  27.5 0.0 copy-done
  27.5 0.0 copy-done.1
  27.5 0.0 copy-done.4
  27.5 0.0 copy-start.2
  27.5 0.0 copy-start.3
  27.6 2.1 %shard_map.121 = (f32[4,64,1024]{2,1,0:T(8,128)S(1)}, f32[1088,128]{1,0:T(8,128)S(1)}) custom-call(s32[1]{0:T(128)} %bitcast.rank_ref, f32[9,64,512]{2,1,0:T(8,128)S(1)} %get-tuple-element.21.local_ref, f32[3,32,128]{2,1,0:T(8,128)S(1)} %bitcast.10, bf16[384,256]{1,0:T(8,128)(2,1)S(1)} %copy-done.4, bf16[576,256]{1,0:T(8,128)(2,1)S(1)} %copy-done, ...), custom_call_target="tpu_custom_call" | custom-call | tf_op jit(solution)/shard_map/pallas_call | solution.py:758
  29.7 29.1 %all_to_all.21 = f32[32,17,2,128]{3,2,1,0:T(2,128)S(1)} all-to-all(f32[32,17,2,128]{3,2,1,0:T(2,128)S(1)} %bitcast.8), channel_id=1, replica_groups=mesh['gx'=8,'gy'=32] {'gy'}, dimensions={0} | all-to-all | bytes 1114112 | tf_op jit(solution)/shard_map/all_to_all | solution.py:765
  58.8 0.0 copy-start.8
  58.8 0.0 copy-start.9
  58.8 2.8 %shard_map.122 = f32[32,32,128]{2,1,0:T(8,128)S(1)} custom-call(f32[1088,128]{1,0:T(8,128)S(1)} %bitcast.7, bf16[256,256]{1,0:T(8,128)(2,1)S(1)} %copy-done.7, bf16[656,256]{1,0:T(8,128)(2,1)S(1)} %copy-done.2, bf16[656,256]{1,0:T(8,128)(2,1)S(1)} %copy-done.3), custom_call_target="tpu_custom_call" | custom-call | tf_op jit(solution)/shard_map/pallas_call | solution.py:766
  61.6 21.6 %all_to_all.22.in_ref = f32[32,32,128]{2,1,0:T(8,128)S(1)} all-to-all(f32[32,32,128]{2,1,0:T(8,128)S(1)} %shard_map.122), channel_id=1, replica_groups=mesh['gx'=8,'gy'=32] {'gy'}, dimensions={0} | all-to-all | bytes 1048576 | tf_op jit(solution)/shard_map/all_to_all | solution.py:772
  83.2 1.9 %shard_map.123 = f32[64,32,128]{2,1,0:T(8,128)} custom-call(f32[4,64,1024]{2,1,0:T(8,128)S(1)} %get-tuple-element.31.local_ref, f32[3,32,128]{2,1,0:T(8,128)S(1)} %bitcast.12, s32[8,128]{1,0:T(8,128)S(1)} %copy-done.9, bf16[576,256]{1,0:T(8,128)(2,1)S(1)} %copy-done, bf16[256,256]{1,0:T(8,128)(2,1)S(1)} %copy-done.8, f32[32,32,128]{2,1,0:T(8,128)S(1)} %all_to_all.22.in_ref), custom_call_target="tpu_custom_call" | custom-call | tf_op jit(solution)/shard_map/pallas_call | solution.py:773
  (7 shorter events, 0.0 us)
Async XLA Ops:
  4.0 12.2 %all-to-all-start = ((f32[8,72,128]{2,1,0:T(8,128)}), f32[8,72,128]{2,1,0:T(8,128)S(1)}, u32[]{:S(2)}, u32[]{:S(2)}) async-start(f32[8,72,128]{2,1,0:T(8,128)} %get-tuple-element.27), calls=%async_computation | async-start | bytes 589824 | tf_op jit(solution)/shard_map/all_to_all | solution.py:738
  8.3 19.2 %copy-start.5 = (f32[3,8,4,128]{3,2,1,0:T(4,128)S(1)}, f32[3,8,4,128]{3,2,1,0:T(4,128)}, u32[]{:S(2)}) copy-start(f32[3,8,4,128]{3,2,1,0:T(4,128)} %param.13) | copy-start | bytes 147460
  8.4 19.2 %copy-start.6 = (f32[3,8,4,128]{3,2,1,0:T(4,128)S(1)}, f32[3,8,4,128]{3,2,1,0:T(4,128)}, u32[]{:S(2)}) copy-start(f32[3,8,4,128]{3,2,1,0:T(4,128)} %param.14) | copy-start | bytes 147460
  13.3 14.2 %copy-start = (bf16[576,256]{1,0:T(8,128)(2,1)S(1)}, bf16[576,256]{1,0:T(8,128)(2,1)}, u32[]{:S(2)}) copy-start(bf16[576,256]{1,0:T(8,128)(2,1)} %get-tuple-element.25.parts_y_ref.parts_ref) | copy-start | bytes 884740
  13.3 14.2 %copy-start.1 = (bf16[704,256]{1,0:T(8,128)(2,1)S(1)}, bf16[704,256]{1,0:T(8,128)(2,1)}, u32[]{:S(2)}) copy-start(bf16[704,256]{1,0:T(8,128)(2,1)} %get-tuple-element.26.from_ref) | copy-start | bytes 1081348
  13.3 14.2 %copy-start.4 = (bf16[384,256]{1,0:T(8,128)(2,1)S(1)}, bf16[384,256]{1,0:T(8,128)(2,1)}, u32[]{:S(2)}) copy-start(bf16[384,256]{1,0:T(8,128)(2,1)} %get-tuple-element.24.parts_ref) | copy-start | bytes 589828
  27.5 31.2 %copy-start.2 = (bf16[656,256]{1,0:T(8,128)(2,1)S(1)}, bf16[656,256]{1,0:T(8,128)(2,1)}, u32[]{:S(2)}) copy-start(bf16[656,256]{1,0:T(8,128)(2,1)} %get-tuple-element.35.up_ref) | copy-start | bytes 1007620
  27.5 31.2 %copy-start.3 = (bf16[656,256]{1,0:T(8,128)(2,1)S(1)}, bf16[656,256]{1,0:T(8,128)(2,1)}, u32[]{:S(2)}) copy-start(bf16[656,256]{1,0:T(8,128)(2,1)} %get-tuple-element.36.down_ref) | copy-start | bytes 1007620
  27.6 31.2 %copy-start.7 = (bf16[256,256]{1,0:T(8,128)(2,1)S(1)}, bf16[256,256]{1,0:T(8,128)(2,1)}, u32[]{:S(2)}) copy-start(bf16[256,256]{1,0:T(8,128)(2,1)} %get-tuple-element.34.gain_ref) | copy-start | bytes 393220
  58.8 24.4 %copy-start.8 = (bf16[256,256]{1,0:T(8,128)(2,1)S(1)}, bf16[256,256]{1,0:T(8,128)(2,1)}, u32[]{:S(2)}) copy-start(bf16[256,256]{1,0:T(8,128)(2,1)} %get-tuple-element.32.from_ref) | copy-start | bytes 393220
  58.8 24.4 %copy-start.9 = (s32[8,128]{1,0:T(8,128)S(1)}, s32[8,128]{1,0:T(8,128)}, u32[]{:S(2)}) copy-start(s32[8,128]{1,0:T(8,128)} %order_ref.1) | copy-start | bytes 12292
